TPU v7x, 256 devices: a whole 4x4x8 slice. The times are simulated.
256 devices in a mesh: grp: 8 (over y, core), seq: 32 (over x, z).
Axes of the slice: x: 4, y: 4, z: 8, core: 2. Of those that a mesh axis runs over, the one named last changes fastest.
Arguments:
- video_queries: bfloat16 [65536, 1536], P(('grp', 'seq')), may hold values from -18 to 18
- audio_keys: bfloat16 [8192, 1536], P(('grp', 'seq')), may hold values from -10 to 10
- audio_values: bfloat16 [8192, 1536], P(('grp', 'seq')), may hold values from -6 to 6
- grad_video: bfloat16 [65536, 1536], P(('grp', 'seq')), may hold values from -6 to 6
- audio_lists: int32 [512, 8], P(('grp', 'seq')), may hold values from -1 to 255, as said below
Outputs:
- grad_queries: bfloat16 [65536, 1536], P(('grp', 'seq'))
- grad_keys: bfloat16 [8192, 1536], P(('grp', 'seq'))
- grad_values: bfloat16 [8192, 1536], P(('grp', 'seq'))
Inputs may be any that keep to these rules, and one draw needn't show every extreme that they name: Each row of audio_lists names 2 to 8 audio blocks that are consecutive numbers in increasing order, followed by -1 entries. Every block named for a video block of device d lies within d - 16 to d + 16.
All inputs are finite; a program needn't handle non-finite values.
Results may differ from a plain program's by a relative error of at most 0.02.
Values may be sent and summed in bfloat16 or wider, within the bound.
A program may use at most 128 MiB of HBM per device.

v0:
```python
import jax
import jax.numpy as jnp
from jax import lax
from jax.sharding import PartitionSpec as P

HEADS = 12


MASKED = -1e30


def extended_2(array, sides, width):
    for axis, dim in sides:
        size, length = (lax.axis_size(axis), array.shape[dim])
        up = [(i, (i + 1) % size) for i in range(size - 1)]
        down = [(j, i) for i, j in up]
        last = lax.slice_in_dim(array, length - width, length, axis=dim)
        initial = lax.slice_in_dim(array, 0, width, axis=dim)
        before = lax.ppermute(last, axis, up)
        after = lax.ppermute(initial, axis, down)
        array = jnp.concatenate([before, array, after], axis=dim)
    return array


def from_behind(value, axis, steps):
    count = lax.axis_size(axis)
    initial, last = (max(0, -steps), min(count, count - steps))
    return lax.ppermute(value, axis, [(source, source + steps) for source in range(initial, last)])


def block_grads(queries, grad_out, key_rows, value_rows, live_keys, head_count):
    blocks, row_count, model_width = queries.shape
    keycount = key_rows.shape[1]
    head_dim = model_width // head_count
    scaling = head_dim ** (-0.5)
    query_heads = queries.reshape(blocks, row_count, head_count, head_dim)
    grad_heads = grad_out.reshape(blocks, row_count, head_count, head_dim)
    key_heads = key_rows.reshape(blocks, keycount, head_count, head_dim)
    value_heads = value_rows.reshape(blocks, keycount, head_count, head_dim)
    scores = (
        jnp.einsum("brhd,bkhd->bhrk", query_heads, key_heads, preferred_element_type=jnp.float32)
        * scaling
    )
    scores = jnp.where(live_keys[:, None, None, :], scores, MASKED)
    row_max = jnp.max(scores, axis=-1, keepdims=True)
    weights = jnp.exp(scores - row_max)
    weights = weights / jnp.sum(weights, axis=-1, keepdims=True)
    weights_low = weights.astype(jnp.bfloat16)
    value_terms = jnp.einsum(
        "bhrk,brhd->bkhd", weights_low, grad_heads, preferred_element_type=jnp.float32
    )
    grad_weights = jnp.einsum(
        "brhd,bkhd->bhrk", grad_heads, value_heads, preferred_element_type=jnp.float32
    )
    row_inner = jnp.sum(weights * grad_weights, axis=-1, keepdims=True)
    grad_scores = (weights * (grad_weights - row_inner) * scaling).astype(jnp.bfloat16)
    grad_queries = jnp.einsum(
        "bhrk,bkhd->brhd", grad_scores, key_heads, preferred_element_type=jnp.float32
    )
    key_terms = jnp.einsum(
        "bhrk,brhd->bkhd", grad_scores, query_heads, preferred_element_type=jnp.float32
    )
    return (
        grad_queries.reshape(blocks, row_count, model_width),
        key_terms.reshape(blocks, keycount, model_width),
        value_terms.reshape(blocks, keycount, model_width),
    )


def per_device(video_queries, audio_keys, audio_values, grad_video, audio_lists):
    audio_rows, model_width = audio_keys.shape
    block_count, list_width = audio_lists.shape
    block_rows = video_queries.shape[0] // block_count
    seq_count = lax.axis_size("seq")
    reach = seq_count // 2
    seq_index = lax.axis_index("seq")
    group_index = lax.axis_index("grp")
    stacked = jnp.stack([audio_keys, audio_values])
    group_panel = lax.all_gather(stacked, "seq", axis=1, tiled=True)
    extended = extended_2(group_panel, (("grp", 1),), reach * audio_rows)
    ext_tiles = extended.reshape(2, extended.shape[1] // audio_rows, audio_rows, model_width)
    base_block = group_index * seq_count - reach
    ext_blocks = ext_tiles.shape[1]
    step_blocks = min(4, block_count)
    step_count = block_count // step_blocks
    valid_slots = audio_lists >= 0
    local_index = jnp.where(valid_slots, audio_lists - base_block, 0)
    query_steps = video_queries.reshape(step_count, step_blocks, block_rows, model_width)
    grad_steps = grad_video.reshape(step_count, step_blocks, block_rows, model_width)
    index_steps = local_index.reshape(step_count, step_blocks, list_width)
    valid_steps = valid_slots.reshape(step_count, step_blocks, list_width)

    def one_step(accumulated, inputs):
        queries, grad_rows, slot_index, slot_valid = inputs
        flat_slots = slot_index.reshape(-1)
        picked = ext_tiles[:, flat_slots].reshape(
            2, step_blocks, list_width * audio_rows, model_width
        )
        live_keys = jnp.repeat(slot_valid, audio_rows, axis=1)
        grad_queries, key_terms, value_terms = block_grads(
            queries, grad_rows, picked[0], picked[1], live_keys, HEADS
        )
        contrib = jnp.stack([key_terms, value_terms]).reshape(
            2, step_blocks * list_width, audio_rows, model_width
        )
        accumulated = accumulated.at[:, flat_slots].add(contrib)
        return (accumulated, grad_queries.astype(jnp.bfloat16))

    initial = jnp.zeros((2, ext_blocks, audio_rows, model_width), jnp.float32)
    accumulated, grad_queries = lax.scan(
        one_step, initial, (query_steps, grad_steps, index_steps, valid_steps)
    )
    rounded = accumulated.astype(jnp.bfloat16)
    own_blocks = rounded[:, reach : reach + seq_count]
    upper_rim = rounded[:, reach + seq_count :]
    lower_rim = rounded[:, :reach]
    zero_blocks = jnp.zeros((2, seq_count - 2 * reach, audio_rows, model_width), jnp.bfloat16)
    rim_blocks = jnp.concatenate([upper_rim, zero_blocks, lower_rim], axis=1)
    own_sum, rim_sum = (
        lax.psum_scatter(
            own_blocks.reshape(2, seq_count * audio_rows, model_width),
            "seq",
            scatter_dimension=1,
            tiled=True,
        ).astype(jnp.float32),
        lax.psum_scatter(
            rim_blocks.reshape(2, seq_count * audio_rows, model_width),
            "seq",
            scatter_dimension=1,
            tiled=True,
        ).astype(jnp.float32),
    )
    from_below = from_behind(
        jnp.where(seq_index < reach, rim_sum, 0.0).astype(jnp.bfloat16), "grp", 1
    ).astype(jnp.float32)
    from_above = from_behind(
        jnp.where(seq_index >= seq_count - reach, rim_sum, 0.0).astype(jnp.bfloat16), "grp", -1
    ).astype(jnp.float32)
    totals = own_sum + from_below + from_above
    return (
        grad_queries.reshape(block_count * block_rows, model_width),
        totals[0].astype(jnp.bfloat16),
        totals[1].astype(jnp.bfloat16),
    )


def solution(mesh):
    placed = (
        P(("grp", "seq"), None),
        P(("grp", "seq"), None),
        P(("grp", "seq"), None),
        P(("grp", "seq"), None),
        P(("grp", "seq"), None),
    )
    return jax.shard_map(
        per_device,
        mesh=mesh,
        in_specs=placed,
        out_specs=(P(("grp", "seq"), None), P(("grp", "seq"), None), P(("grp", "seq"), None)),
        check_vma=False,
    )
```

profile of v0, /device:TPU:8, one launch (start us, length us, event | category | flops | bytes accessed | tf_op | source)
XLA Modules:
  0.0 712.3 jit_solution(4663844195762829295)
XLA Ops:
  7.2 0.0 all-gather.2.cloned.1.call-start
  7.2 1.6 pad_maximum_fusion.2
  8.8 0.0 all-gather.2.cloned.1.call-update
  8.9 0.0 copy-start.5
  8.9 0.0 reduce-scatter.5.cloned.1.call-start
  8.9 93.8 %all-gather.2.cloned.1.call-done = bf16[2,1024,1536]{2,1,0:T(8,128)(2,1)} async-done(((bf16[2,32,1536]{2,1,0:T(8,128)(2,1)}), bf16[2,1024,1536]{2,1,0:T(8,128)(2,1)}) %all-gather.2.cloned.1.call-update) | async-done | bytes 6291472 | tf_op jit(solution)/shard_map/all_gather | solution.py:79
  102.8 5.9 fusion.32
  108.7 1.9 collective-permute-start.1
  110.6 2.4 collective-permute-start
  113.0 0.0 copy-done.5
  113.0 0.1 reshape.99
  113.1 2.4 reshape.122
  115.5 2.4 reshape.121
  117.9 0.1 broadcast_in_dim.45
  118.0 0.1 broadcast_in_dim.46
  118.1 27.6 %collective-permute-done.1 = bf16[2,512,1536]{2,1,0:T(8,128)(2,1)S(1)} collective-permute-done((bf16[2,512,1536]{2,1,0:T(8,128)(2,1)}, bf16[2,512,1536]{2,1,0:T(8,128)(2,1)S(1)}, u32[]{:S(2)}, u32[]{:S(2)}) %collective-permute-start.1) | collective-permute-done | bytes 3145760 | tf_op jit(solution)/shard_map/ppermute | solution.py:20
  145.7 3.8 collective-permute-done
  149.5 9.3 %pad_maximum_fusion = bf16[2,2048,1536]{2,1,0:T(8,128)(2,1)} fusion(bf16[2,512,1536]{2,1,0:T(8,128)(2,1)S(1)} %collective-permute-done.1, bf16[2,1024,1536]{2,1,0:T(8,128)(2,1)} %all-gather.2.cloned.1.call-done, bf16[2,512,1536]{2,1,0:T(8,128)(2,1)} %collective-permute-done), kind=kLoop, calls=%fused_computation.4 | loop fusion | flops 37748736 | bytes 25165824 | tf_op jit(solution)/shard_map/concatenate | solution.py:21
  158.8 5.3 gather_fusion
  164.1 1.9 fusion.33
  166.0 2.9 squeeze.21
  168.9 0.0 copy-start.4
  168.9 2.7 copy.34
  171.6 2.9 squeeze.22
  174.5 0.0 copy-done.4
  174.5 0.0 copy-start.1
  174.5 0.0 copy-start.3
  174.5 2.2 fusion.9
  176.7 0.0 copy-done.3
  176.7 0.6 fusion.20
  177.4 1.2 fusion.34
  178.6 0.6 convolution_bitcast_fusion
  179.2 1.1 copy-done.6
  180.4 3.8 copy.40
  184.1 3.0 stack.21
  187.2 8.1 %convolution_bitcast_fusion.1 = f32[2,256,12,128]{3,1,2,0:T(8,128)} fusion(f32[2,12,256,128]{3,2,1,0:T(8,128)} %fusion.9, bf16[2,128,12,128]{3,2,1,0:T(8,128)(2,1)} %reshape.121, f32[2,12,128,256]{2,3,1,0:T(8,128)} %copy-done.6, f32[2,12,128]{2,1,0:T(8,128)S(1)} %get-tuple-element.43), kind=kOutput, calls=%fused_computation.18 | convolution fusion | flops 206834944 | bytes 10235904 | tf_op jit(solution)/shard_map/while/body/eval_jaxpr/bhrk,brhd->bkhd/dot_general | solution.py:60
  195.2 5.7 copy.38
  200.9 4.7 stack.20
  205.6 2.3 maximum_bitcast_fusion
  207.9 3.1 copy.41
  211.0 11.5 %broadcast_in_dim.49 = f32[2,64,32,1536]{3,2,1,0:T(8,128)} broadcast(f32[]{:T(128)} %constant.47.clone.1), dimensions={} | broadcast | bytes 25165828 | tf_op jit(solution)/shard_map/broadcast_in_dim | solution.py:109
  222.6 15.1 %scatter_fusion = f32[2,64,32,1536]{3,2,1,0:T(8,128)} fusion(f32[2,64,32,1536]{3,2,1,0:T(8,128)} %broadcast_in_dim.49, s32[16]{0:T(128)S(1)} %fusion.24, f32[16,2,32,1536]{3,2,1,0:T(8,128)} %copy.41), kind=kCustom, calls=%fused_computation.1 | custom fusion | flops 1572864 | bytes 18874432 | tf_op jit(solution)/shard_map/while/body/eval_jaxpr/scatter-add | solution.py:106
  237.7 9.4 %convert_element_type.53 = bf16[2,64,32,1536]{3,2,1,0:T(8,128)(2,1)S(1)} convert(f32[2,64,32,1536]{3,2,1,0:T(8,128)} %scatter_fusion) | non-fusion elementwise | flops 6291456 | bytes 37748736 | tf_op jit(solution)/shard_map/convert_element_type | solution.py:113
  247.1 0.0 copy-start
  247.1 0.4 fusion.31
  247.5 4.1 copy-done
  251.6 3.1 pad_maximum_fusion.1
  254.8 0.0 reduce-scatter.5.cloned.1.call-update
  254.8 0.0 reduce-scatter.3.cloned.1.call-start
  254.9 6.1 slice.48
  261.0 0.0 reduce-scatter.3.cloned.1.call-update
  261.0 215.6 %reduce-scatter.5.cloned.1.call-done = bf16[2,32,1536]{2,1,0:T(8,128)(2,1)} async-done(((bf16[2,1024,1536]{2,1,0:T(8,128)(2,1)}), bf16[2,32,1536]{2,1,0:T(8,128)(2,1)}) %reduce-scatter.5.cloned.1.call-update) | async-done | bytes 196624 | tf_op jit(solution)/shard_map/reduce_scatter | solution.py:126
  476.6 1.0 fusion.22
  477.6 1.9 collective-permute-start.3
  479.5 2.4 collective-permute-start.2
  482.0 0.0 copy-done.2
  482.0 6.1 fusion.16
  488.1 0.9 copy.44
  489.1 1.1 copy.62
  490.1 213.9 %reduce-scatter.3.cloned.1.call-done = bf16[2,32,1536]{2,1,0:T(8,128)(2,1)} async-done(((bf16[2,1024,1536]{2,1,0:T(8,128)(2,1)}), bf16[2,32,1536]{2,1,0:T(8,128)(2,1)}) %reduce-scatter.3.cloned.1.call-update) | async-done | bytes 196624 | tf_op jit(solution)/shard_map/reduce_scatter | solution.py:120
  704.1 0.0 collective-permute-done.3
  704.1 0.0 collective-permute-done.2
  704.1 1.0 add_convert_fusion
  705.1 0.7 slice_bitcast_fusion
  (7 shorter events, 0.0 us)
Async XLA Ops:
  7.2 95.6 %all-gather.2.cloned.1.call-start = ((), (), s32[]{:S(2)}) async-start(), calls=%async_computation.2 | async-start | bytes 6488064 | tf_op jit(solution)/shard_map/all_gather | solution.py:79
  8.9 104.1 %copy-start.5 = (s32[2,8]{1,0:T(2,128)S(1)}, s32[2,8]{1,0:T(2,128)}, u32[]{:S(2)}) copy-start(s32[2,8]{1,0:T(2,128)} %param.9) | copy-start | bytes 196
  8.9 467.7 %reduce-scatter.5.cloned.1.call-start = ((), (), s32[]{:S(2)}) async-start(), calls=%async_computation.4 | async-start | bytes 6488064 | tf_op jit(solution)/shard_map/reduce_scatter | solution.py:126
  108.7 37.0 %collective-permute-start.1 = (bf16[2,512,1536]{2,1,0:T(8,128)(2,1)}, bf16[2,512,1536]{2,1,0:T(8,128)(2,1)S(1)}, u32[]{:S(2)}, u32[]{:S(2)}) collective-permute-start(bf16[2,512,1536]{2,1,0:T(8,128)(2,1)} %get-tuple-element.36), channel_id=1, source_target_pairs={{32,0},{64,32},{96,64},{128,96},{160,128},{192,160},{224,192},{33,... | collective-permute-start | bytes 9437192 | tf_op jit(solution)/shard_map/ppermute | solution.py:20
  110.6 38.9 %collective-permute-start = (bf16[2,512,1536]{2,1,0:T(8,128)(2,1)}, bf16[2,512,1536]{2,1,0:T(8,128)(2,1)}, u32[]{:S(2)}, u32[]{:S(2)}) collective-permute-start(bf16[2,512,1536]{2,1,0:T(8,128)(2,1)} %get-tuple-element.35), channel_id=1, source_target_pairs={{0,32},{32,64},{64,96},{96,128},{128,160},{160,192},{192,224},{1,3... | collective-permute-start | bytes 9437192 | tf_op jit(solution)/shard_map/ppermute | solution.py:19
  168.9 5.6 copy-start.4
  174.5 2.2 copy-start.1
  174.5 2.2 copy-start.3
  178.6 1.7 copy-start.6
  247.1 4.5 copy-start
  254.8 449.3 %reduce-scatter.3.cloned.1.call-start = ((), (), s32[]{:S(2)}) async-start(), calls=%async_computation.3 | async-start | bytes 6488064 | tf_op jit(solution)/shard_map/reduce_scatter | solution.py:120
  261.0 221.0 %copy-start.2 = (bf16[2,256,12,128]{1,3,2,0:T(8,128)(2,1)S(1)}, bf16[2,256,12,128]{1,3,2,0:T(8,128)(2,1)}, u32[]{:S(2)}) copy-start(bf16[2,256,12,128]{1,3,2,0:T(8,128)(2,1)} %copy.34) | copy-start | bytes 4718596
  477.6 226.5 %collective-permute-start.3 = (bf16[2,32,1536]{2,1,0:T(8,128)(2,1)S(1)}, bf16[2,32,1536]{2,1,0:T(8,128)(2,1)S(1)}, u32[]{:S(2)}, u32[]{:S(2)}) collective-permute-start(bf16[2,32,1536]{2,1,0:T(8,128)(2,1)S(1)} %get-tuple-element.42), channel_id=1, source_target_pairs={{32,0},{64,32},{96,64},{128,96},{160,128},{192,160},{224,192},{33,... | collective-permute-start | bytes 589832 | tf_op jit(solution)/shard_map/ppermute | solution.py:28
  479.5 224.5 %collective-permute-start.2 = (bf16[2,32,1536]{2,1,0:T(8,128)(2,1)S(1)}, bf16[2,32,1536]{2,1,0:T(8,128)(2,1)S(1)}, u32[]{:S(2)}, u32[]{:S(2)}) collective-permute-start(bf16[2,32,1536]{2,1,0:T(8,128)(2,1)S(1)} %get-tuple-element.41), channel_id=1, source_target_pairs={{0,32},{32,64},{64,96},{96,128},{128,160},{160,192},{192,224},{1,3... | collective-permute-start | bytes 589832 | tf_op jit(solution)/shard_map/ppermute | solution.py:28
Sparse Core Ops, SparseCore 0:
  11.2 91.5 all-gather.1
  254.9 221.6 reduce-scatter.4
  481.1 222.8 reduce-scatter.2
where the time goes:
time: 713 us; the launch traced here: 712 us
  waiting for transfers between devices  555 us (78%)
  local copies, waits for them, and re-layouts  72.9 us (10%)
  other arithmetic  44.1 us (6%)
  matrix products  17.6 us (2%)
  between operations  14 us (2%)
  starting transfers between devices  8.76 us (1%)
    reduce_scatter x1, waiting for transfers between devices, per_device(): lax.psum_scatter(rim_blocks.reshape(2, seq_count * audio_rows, model_widt...  216 us
    reduce_scatter x1, waiting for transfers between devices, per_device(): lax.psum_scatter(own_blocks.reshape(2, seq_count * audio_rows, model_widt...  214 us
    all_gather x1, waiting for transfers between devices, per_device(): group_panel = lax.all_gather(stacked, 'seq', axis=1, tiled=True)  93.8 us
    ppermute x1, waiting for transfers between devices, extended_2(): after = lax.ppermute(initial, axis, down)  27.6 us
    scatter-add x1, other arithmetic, one_step(): accumulated = accumulated.at[:, flat_slots].add(contrib)  15.1 us
  transfers between devices with their start and end apart: 7, of which 5 were waited for; matrix products, arithmetic and copies ran while one was open for 3% of the time, Pallas kernels for 0%

commit v1 on v0

v1 whole, which is shorter than its diff:
```python
import functools

import jax
import jax.numpy as jnp
from jax import lax
from jax.experimental import pallas as pl
from jax.experimental.pallas import tpu as pltpu
from jax.sharding import PartitionSpec as P

MESH = pl.DeviceIdType.MESH
HEADS = 12
HDIM = 128
NX, NZ, NC = 4, 8, 8
HPD = HEADS // NX
COLS = HPD * HDIM
ROWS = 32
VROWS = 256
VBLK = 128
KEYS = 256
WIN = 2 * NX * NZ
MASKED = -1e30


def position():
    c, s = lax.axis_index("grp"), lax.axis_index("seq")
    return c, s // NZ, s % NZ


def dev(c, x, z):
    return {"grp": c, "seq": x * NZ + z}


def enter(c, x, z):
    barrier = pltpu.get_barrier_semaphore()

    def greet(*where):
        pl.semaphore_signal(barrier, inc=1, device_id=dev(*where), device_id_type=MESH)

    for r in range(1, NX):
        greet(c, (x + r) % NX, z)
    greet(c, x, (z + 1) % NZ)
    greet(c, x, (z + NZ - 1) % NZ)

    @pl.when(c > 0)
    def _():
        greet(c - 1, x, z)

    @pl.when(c < NC - 1)
    def _():
        greet(c + 1, x, z)

    inner = jnp.logical_and(c > 0, c < NC - 1)
    pl.semaphore_wait(barrier, NX - 1 + 2 + 1 + inner.astype(jnp.int32))


def remote(src, dst, sems, at, where):
    return pltpu.make_async_remote_copy(
        src_ref=src,
        dst_ref=dst,
        send_sem=sems[0].at[at],
        recv_sem=sems[1].at[at],
        device_id=dev(*where),
        device_id_type=MESH,
    )


def cols_of(x):
    return pl.ds(pl.multiple_of(x * COLS, COLS), COLS)


def gather_kernel(
    q, g, k, v, info, qg, kv, infos,
    x_send, x_recv, i_send, i_recv, v_send, v_recv, r_send, r_recv, e_send, e_recv, own,
):
    c, x, z = position()
    enter(c, x, z)
    audio, video = (k, v), (q, g)

    started = []

    def go(copy):
        copy.start()
        started.append(copy)
        return copy

    locals_ = []
    for w in range(2):
        copy = pltpu.make_async_copy(audio[w].at[:, cols_of(x)], kv.at[w, 2 + x, z], own.at[w])
        copy.start()
        locals_.append(copy)
    for w in range(2):
        for r in range(1, NX):
            to = (x + r) % NX
            go(remote(audio[w].at[:, cols_of(to)], kv.at[w, 2 + x, z], (x_send, x_recv), (w, r - 1), (c, to, z)))
    for r in range(1, NX):
        go(remote(info, infos.at[x], (i_send, i_recv), r - 1, (c, (x + r) % NX, z)))
    for w in range(2):
        for r in range(1, NX):
            to = (x + r) % NX
            go(remote(video[w].at[:, cols_of(to)], qg.at[w, x], (v_send, v_recv), (w, r - 1), (c, to, z)))
    late = [pltpu.make_async_copy(info, infos.at[x], own.at[4])]
    for w in range(2):
        late.append(pltpu.make_async_copy(video[w].at[:, cols_of(x)], qg.at[w, x], own.at[2 + w]))
    for copy in late:
        copy.start()

    def spread(w, rel):
        zz = (z + rel) % NZ
        up = remote(kv.at[w, pl.ds(4, 2), zz], kv.at[w, pl.ds(0, 2), zz], (e_send, e_recv), (w, 0, rel), (jnp.minimum(c + 1, NC - 1), x, z))
        down = remote(kv.at[w, pl.ds(2, 2), zz], kv.at[w, pl.ds(6, 2), zz], (e_send, e_recv), (w, 1, rel), (jnp.maximum(c - 1, 0), x, z))
        return up, down

    def ring(w, d, step):
        sign = 1 - 2 * d
        panel = kv.at[w, pl.ds(2, NX), (z - sign * step + NZ) % NZ]
        return remote(panel, panel, (r_send, r_recv), (w, d, step), (c, x, (z + sign + NZ) % NZ))

    def arrived(w, d, step):
        sign = 1 - 2 * d
        panel = kv.at[w, pl.ds(2, NX), (z - sign * (step + 1) + 2 * NZ) % NZ]
        remote(panel, panel, (r_send, r_recv), (w, d, step), (c, x, (z + sign + NZ) % NZ)).wait_recv()

    def spread_start(w, rel):
        up, down = spread(w, rel)

        @pl.when(c < NC - 1)
        def _():
            up.start()

        @pl.when(c > 0)
        def _():
            down.start()

    for w in range(2):
        locals_[w].wait()
        for r in range(1, NX):
            came = (x - r + NX) % NX
            remote(audio[w].at[:, cols_of(x)], kv.at[w, 2 + came, z], (x_send, x_recv), (w, r - 1), (c, came, z)).wait_recv()
        for d in range(2):
            go(ring(w, d, 0))
        spread_start(w, 0)
    for step in range(1, 5):
        for w in range(2):
            for d in range(2):
                if step == 4 and w != d:
                    continue
                arrived(w, d, step - 1)
                if step < 3 or (step == 3 and w == d):
                    go(ring(w, d, step))
                spread_start(w, (-step if d == 0 else step) % NZ)

    for copy in late:
        copy.wait()
    for r in range(1, NX):
        came = (x - r + NX) % NX
        remote(info, infos.at[came], (i_send, i_recv), r - 1, (c, came, z)).wait_recv()
        for w in range(2):
            remote(video[w].at[:, cols_of(x)], qg.at[w, came], (v_send, v_recv), (w, r - 1), (c, came, z)).wait_recv()
    for w in range(2):
        for rel in range(NZ):
            up, down = spread(w, rel)

            @pl.when(c < NC - 1)
            def _():
                up.wait_send()
                remote(kv.at[w, pl.ds(6, 2), (z + rel) % NZ], kv.at[w, pl.ds(6, 2), (z + rel) % NZ], (e_send, e_recv), (w, 1, rel), (jnp.minimum(c + 1, NC - 1), x, z)).wait_recv()

            @pl.when(c > 0)
            def _():
                down.wait_send()
                remote(kv.at[w, pl.ds(0, 2), (z + rel) % NZ], kv.at[w, pl.ds(0, 2), (z + rel) % NZ], (e_send, e_recv), (w, 0, rel), (jnp.maximum(c - 1, 0), x, z)).wait_recv()
    for copy in started:
        copy.wait_send()


def nt(a, b):
    return lax.dot_general(a, b, (((1,), (1,)), ((), ())), preferred_element_type=jnp.float32)


def tn(a, b):
    return lax.dot_general(a, b, (((0,), (0,)), ((), ())), preferred_element_type=jnp.float32)


def nn(a, b):
    return lax.dot_general(a, b, (((1,), (0,)), ((), ())), preferred_element_type=jnp.float32)


def compute_kernel(info, qg, kv, dq, out, acc):
    scale = HDIM**-0.5
    acc[...] = jnp.zeros_like(acc)
    key_at = lax.broadcasted_iota(jnp.int32, (KEYS, VBLK), 0)

    def tile(t, _):
        row = (t // 2) * 8 + t % 2
        first = pl.multiple_of(info[row, 0] * ROWS, ROWS)
        live = jnp.logical_and(key_at >= info[row, 1] * ROWS, key_at < info[row, 2] * ROWS)
        rows = pl.ds(pl.multiple_of(t * VBLK, VBLK), VBLK)
        keys = pl.ds(first, KEYS)
        for h in range(HPD):
            cols = pl.ds(h * HDIM, HDIM)
            qt, gt = qg[0, rows, cols], qg[1, rows, cols]
            kt, vt = kv[0, keys, cols], kv[1, keys, cols]
            scores = jnp.where(live, nt(kt, qt) * scale, MASKED)
            raw = jnp.exp(scores - jnp.max(scores, axis=0, keepdims=True))
            weights = raw * (1.0 / jnp.sum(raw, axis=0, keepdims=True))
            grad_weights = nt(vt, gt)
            inner = jnp.sum(weights * grad_weights, axis=0, keepdims=True)
            grad_scores = (weights * (grad_weights - inner) * scale).astype(jnp.bfloat16)
            acc[1, keys, cols] += nn(weights.astype(jnp.bfloat16), gt)
            acc[0, keys, cols] += nn(grad_scores, qt)
            dq[rows, cols] = tn(grad_scores, kt).astype(jnp.bfloat16)
        return 0

    lax.fori_loop(0, 2 * NX, tile, 0)
    out[...] = acc[...].astype(jnp.bfloat16)


def reduce_kernel(
    dq, part, out_q, out_k, out_v,
    edge, moving, landed, final,
    q_send, q_recv, e_send, e_recv, r_send, r_recv, f_send, f_recv, own,
):
    c, x, z = position()
    enter(c, x, z)
    outs = (out_k, out_v)
    started = []

    def go(copy):
        copy.start()
        started.append(copy)
        return copy

    def edges(w, rel):
        zz = (z + rel) % NZ
        up = remote(part.at[w, pl.ds(6, 2), zz], edge.at[w, 0, rel], (e_send, e_recv), (w, 0, rel), (jnp.minimum(c + 1, NC - 1), x, z))
        down = remote(part.at[w, pl.ds(0, 2), zz], edge.at[w, 1, rel], (e_send, e_recv), (w, 1, rel), (jnp.maximum(c - 1, 0), x, z))
        return up, down

    order = (4, 3, 5, 2, 6, 1, 7, 0)
    for rel in order:
        for w in range(2):
            up, down = edges(w, rel)

            @pl.when(c < NC - 1)
            def _():
                up.start()

            @pl.when(c > 0)
            def _():
                down.start()

    @pl.when(c == 0)
    def _():
        edge[:, 0] = jnp.zeros((2,) + edge.shape[2:], edge.dtype)

    @pl.when(c == NC - 1)
    def _():
        edge[:, 1] = jnp.zeros((2,) + edge.shape[2:], edge.dtype)

    for r in range(1, NX):
        to = (x + r) % NX
        go(remote(dq.at[to], out_q.at[:, cols_of(x)], (q_send, q_recv), r - 1, (c, to, z)))
    own_q = pltpu.make_async_copy(dq.at[x], out_q.at[:, cols_of(x)], own.at[2])
    own_q.start()

    def total(w, rel):
        @pl.when(c < NC - 1)
        def _():
            edges(w, rel)[1].wait_recv()

        @pl.when(c > 0)
        def _():
            edges(w, rel)[0].wait_recv()

        mine = part[w, pl.ds(2, NX), (z + rel) % NZ].astype(jnp.float32)
        low = edge[w, 0, rel].astype(jnp.float32)
        high = edge[w, 1, rel].astype(jnp.float32)
        return mine + jnp.concatenate([low, high], axis=0)

    def ring(w, d, dist):
        sign = 1 - 2 * d
        at = (w, d, dist - 1)
        return remote(moving.at[at], landed.at[at], (r_send, r_recv), at, (c, x, (z + sign + NZ) % NZ))

    for dist in range(4, 0, -1):
        for w in range(2):
            for d in range(2):
                if dist == 4 and w != d:
                    continue
                value = total(w, (dist if d == 0 else -dist) % NZ)
                if dist < 3 or (dist == 3 and w == d):
                    ring(w, d, dist + 1).wait_recv()
                    value = value + landed[w, d, dist].astype(jnp.float32)
                moving[w, d, dist - 1] = value.astype(jnp.bfloat16)
                go(ring(w, d, dist))

    def last(w, to, at):
        return remote(final.at[w, to], outs[w].at[:, cols_of(x)], (f_send, f_recv), (w, at), (c, to, z))

    kept = []
    for w in range(2):
        value = total(w, 0)
        for d in range(2):
            ring(w, d, 1).wait_recv()
            value = value + landed[w, d, 0].astype(jnp.float32)
        final[w] = value.astype(jnp.bfloat16)
        for r in range(1, NX):
            go(last(w, (x + r) % NX, r - 1))
        copy = pltpu.make_async_copy(final.at[w, x], outs[w].at[:, cols_of(x)], own.at[w])
        copy.start()
        kept.append(copy)

    own_q.wait()
    for r in range(1, NX):
        came = (x - r + NX) % NX
        remote(dq.at[0], out_q.at[:, cols_of(came)], (q_send, q_recv), r - 1, (c, came, z)).wait_recv()
        for w in range(2):
            remote(final.at[w, 0], outs[w].at[:, cols_of(came)], (f_send, f_recv), (w, r - 1), (c, came, z)).wait_recv()
    for copy in kept:
        copy.wait()
    for w in range(2):
        for rel in range(NZ):
            up, down = edges(w, rel)

            @pl.when(c < NC - 1)
            def _():
                up.wait_send()

            @pl.when(c > 0)
            def _():
                down.wait_send()
    for copy in started:
        copy.wait_send()


ANY = pl.BlockSpec(memory_space=pl.ANY)
VMEM = pl.BlockSpec(memory_space=pltpu.VMEM)
SMEM = pl.BlockSpec(memory_space=pltpu.SMEM)


def sems(*shape):
    return [pltpu.SemaphoreType.DMA(shape)] * 2


def shaped(shape, dtype=jnp.bfloat16):
    return jax.ShapeDtypeStruct(shape, dtype)


def per_device(q, k, v, g, lists):
    c = lax.axis_index("grp")
    first = lists[:, 0] - (c * NX * NZ - WIN // 4)
    count = jnp.sum((lists >= 0).astype(jnp.int32), axis=1)
    highest = jnp.where(c == NC - 1, WIN * 3 // 4, WIN) - 8
    base = jnp.minimum(first, highest)
    info = jnp.stack([base, first - base, first - base + count], axis=1)
    info = jnp.pad(info, ((0, 6), (0, 125)))

    qg, kv, infos = pl.pallas_call(
        gather_kernel,
        out_shape=(
            shaped((2, NX, VROWS, COLS)),
            shaped((2, 8, NZ, ROWS, COLS)),
            shaped((NX, 8, 128), jnp.int32),
        ),
        in_specs=[ANY] * 5,
        out_specs=(ANY,) * 3,
        scratch_shapes=[
            *sems(2, NX - 1), *sems(NX - 1), *sems(2, NX - 1), *sems(2, 2, 4), *sems(2, 2, NZ),
            pltpu.SemaphoreType.DMA((5,)),
        ],
        compiler_params=pltpu.CompilerParams(collective_id=0, has_side_effects=True),
        name="gather",
    )(q, g, k, v, info)

    dq, part = pl.pallas_call(
        compute_kernel,
        out_shape=(shaped((NX * VROWS, COLS)), shaped((2, WIN * ROWS, COLS))),
        in_specs=[SMEM, VMEM, VMEM],
        out_specs=(VMEM, VMEM),
        scratch_shapes=[pltpu.VMEM((2, WIN * ROWS, COLS), jnp.float32)],
        compiler_params=pltpu.CompilerParams(vmem_limit_bytes=40 * 2**20),
        name="compute",
    )(
        infos.reshape(NX * 8, 128),
        qg.reshape(2, NX * VROWS, COLS),
        kv.reshape(2, WIN * ROWS, COLS),
    )

    return pl.pallas_call(
        reduce_kernel,
        out_shape=(shaped(q.shape), shaped(k.shape), shaped(v.shape)),
        in_specs=[ANY, VMEM],
        out_specs=(ANY,) * 3,
        scratch_shapes=[
            pltpu.VMEM((2, 2, NZ, 2, ROWS, COLS), jnp.bfloat16),
            pltpu.VMEM((2, 2, 4, NX, ROWS, COLS), jnp.bfloat16),
            pltpu.VMEM((2, 2, 4, NX, ROWS, COLS), jnp.bfloat16),
            pltpu.VMEM((2, NX, ROWS, COLS), jnp.bfloat16),
            *sems(NX - 1), *sems(2, 2, NZ), *sems(2, 2, 4), *sems(2, NX - 1),
            pltpu.SemaphoreType.DMA((3,)),
        ],
        compiler_params=pltpu.CompilerParams(
            collective_id=1, has_side_effects=True, vmem_limit_bytes=40 * 2**20
        ),
        name="reduce",
    )(dq.reshape(NX, VROWS, COLS), part.reshape(2, 8, NZ, ROWS, COLS))


def solution(mesh):
    placed = P(("grp", "seq"), None)
    return jax.shard_map(
        per_device,
        mesh=mesh,
        in_specs=(placed,) * 5,
        out_specs=(placed,) * 3,
        check_vma=False,
    )
```

time: 713 us -> 87.1 us (0.12)
  waiting for transfers between devices: 555 us -> 0 us
  Pallas kernels: 0 us -> 77.8 us
  local copies, waits for them, and re-layouts: 72.9 us -> 6.87 us
  other arithmetic: 44.1 us -> 1.56 us
  matrix products: 17.6 us -> 0 us
  between operations: 14 us -> 0.68 us
  starting transfers between devices: 8.76 us -> 0 us
    reduce_scatter x2 -> x0, waiting for transfers between devices: 430 us -> none  [the longest x1 216 us: per_device(): lax.psum_scatter(rim_blocks.reshape(2, seq_count * audio_rows, model_widt...]
    all_gather x1 -> x0, waiting for transfers between devices: 93.8 us -> none  [per_device(): group_panel = lax.all_gather(stacked, 'seq', axis=1, tiled=True)]
    pallas_call x0 -> x3, Pallas kernels: none -> 77.8 us  [the longest x1 35.6 us: per_device(): pl.pallas_call(gather_kernel, out_shape=(shaped((2, NX, VROWS, COLS)), sh...]
    ppermute x4 -> x0, waiting for transfers between devices: 31.4 us -> none  [the longest x1 27.6 us: extended_2(): after = lax.ppermute(initial, axis, down)]
    dot_general x5 -> x0, matrix products: 17.6 us -> none  [the longest x1 8.05 us: block_grads(): jnp.einsum('bhrk,brhd->bkhd', grad_scores, query_heads, preferred_element...]
    scatter-add x1 -> x0, other arithmetic: 15.1 us -> none  [one_step(): accumulated = accumulated.at[:, flat_slots].add(contrib)]
    slice x4 -> x0, local copies, waits for them, and re-layouts: 14.3 us -> none  [the longest x1 6.13 us: per_device(): own_blocks = rounded[:, reach:reach + seq_count]]
    concatenate x2 -> x0, other arithmetic: 12.4 us -> none  [the longest x1 9.3 us: extended_2(): array = jnp.concatenate([before, array, after], axis=dim)]
  transfers between devices with their start and end apart: 7 -> 0, of which waited for: 5 -> 0; matrix products, arithmetic and copies ran while one was open for 3% -> 0% of each run, Pallas kernels for 0% -> 0%
where the time goes in v1:
time: 87.1 us; the launch traced here: 86.9 us
  Pallas kernels  77.8 us (89%)
  local copies, waits for them, and re-layouts  6.87 us (8%)
  other arithmetic  1.56 us (2%)
    pallas_call x1, Pallas kernels, per_device(): pl.pallas_call(gather_kernel, out_shape=(shaped((2, NX, VROWS, COLS)), sh...  35.6 us
    pallas_call x1, Pallas kernels, per_device(): pl.pallas_call(reduce_kernel, out_shape=(shaped(q.shape), shaped(k.shape)...  31.4 us
    pallas_call x1, Pallas kernels, per_device(): pl.pallas_call(compute_kernel, out_shape=(shaped((NX * VROWS, COLS)), sha...  10.7 us
    unnamed x9, local copies, waits for them, and re-layouts  6.17 us

profile of v1, /device:TPU:8, one launch (start us, length us, event | category | flops | bytes accessed | tf_op | source)
XLA Modules:
  0.0 86.9 jit_solution(8277012579668929164)
XLA Ops:
  0.6 0.8 fusion
  1.4 0.1 copy.8
  1.5 0.7 fusion.3
  2.2 0.1 pad_add_fusion
  2.3 0.6 pad.4.info
  2.9 35.6 %gather.1 = (bf16[2,4,256,384]{3,2,1,0:T(8,128)(2,1)}, bf16[2,8,8,32,384]{4,3,2,1,0:T(8,128)(2,1)}, s32[4,8,128]{2,1,0:T(8,128)}) custom-call(bf16[256,1536]{1,0:T(8,128)(2,1)} %q.1, bf16[256,1536]{1,0:T(8,128)(2,1)} %g.1, bf16[32,1536]{1,0:T(8,128)(2,1)} %k.1, bf16[32,1536]{1,0:T(8,128)(2,1)} %v.1, s32[8,128]{1,0:T(8,128)} %pad.4.info), custom_call_target="tpu_custom_call" | custom-call | tf_op jit(solution)/shard_map/gather/pallas_call | solution.py:358
  38.5 0.0 copy-start
  38.5 1.9 %copy-done = bf16[2,8,8,32,384]{4,3,2,1,0:T(8,128)(2,1)S(1)} copy-done((bf16[2,8,8,32,384]{4,3,2,1,0:T(8,128)(2,1)S(1)}, bf16[2,8,8,32,384]{4,3,2,1,0:T(8,128)(2,1)}, u32[]{:S(2)}) %copy-start) | copy-done | bytes 3145752
  40.4 0.0 copy-start.1
  40.4 1.4 %copy-done.1 = bf16[2,4,256,384]{3,2,1,0:T(8,128)(2,1)S(1)} copy-done((bf16[2,4,256,384]{3,2,1,0:T(8,128)(2,1)S(1)}, bf16[2,4,256,384]{3,2,1,0:T(8,128)(2,1)}, u32[]{:S(2)}) %copy-start.1) | copy-done | bytes 1572888
  41.8 0.0 copy-start.2
  41.8 0.7 copy-done.2
  42.6 10.7 %compute.1 = (bf16[1024,384]{1,0:T(8,128)(2,1)S(1)}, bf16[2,2048,384]{2,1,0:T(8,128)(2,1)S(1)}) custom-call(s32[32,128]{1,0:T(8,128)S(1)} %bitcast.10, bf16[2,1024,384]{2,1,0:T(8,128)(2,1)S(1)} %bitcast.8, bf16[2,2048,384]{2,1,0:T(8,128)(2,1)S(1)} %bitcast.6), custom_call_target="tpu_custom_call" | custom-call | tf_op jit(solution)/shard_map/compute/pallas_call | solution.py:375
  53.3 31.4 %reduce.1 = (bf16[256,1536]{1,0:T(8,128)(2,1)S(1)}, bf16[32,1536]{1,0:T(8,128)(2,1)S(1)}, bf16[32,1536]{1,0:T(8,128)(2,1)S(1)}) custom-call(bf16[4,256,384]{2,1,0:T(8,128)(2,1)S(1)} %bitcast.9, bf16[2,8,8,32,384]{4,3,2,1,0:T(8,128)(2,1)S(1)} %bitcast.7), custom_call_target="tpu_custom_call" | custom-call | tf_op jit(solution)/shard_map/reduce/pallas_call | solution.py:389
  84.7 0.9 %copy.12 = bf16[256,1536]{1,0:T(8,128)(2,1)} copy(bf16[256,1536]{1,0:T(8,128)(2,1)S(1)} %get-tuple-element.19) | data formatting | bytes 1572864
  85.6 0.6 copy.13
  86.2 0.6 copy.14
Async XLA Ops:
  38.5 1.9 %copy-start = (bf16[2,8,8,32,384]{4,3,2,1,0:T(8,128)(2,1)S(1)}, bf16[2,8,8,32,384]{4,3,2,1,0:T(8,128)(2,1)}, u32[]{:S(2)}) copy-start(bf16[2,8,8,32,384]{4,3,2,1,0:T(8,128)(2,1)} %get-tuple-element.10) | copy-start | bytes 9437188
  40.4 1.4 %copy-start.1 = (bf16[2,4,256,384]{3,2,1,0:T(8,128)(2,1)S(1)}, bf16[2,4,256,384]{3,2,1,0:T(8,128)(2,1)}, u32[]{:S(2)}) copy-start(bf16[2,4,256,384]{3,2,1,0:T(8,128)(2,1)} %get-tuple-element.9) | copy-start | bytes 4718596
  41.8 0.7 copy-start.2

commit v2 on v0

v2 whole, which is shorter than its diff:
```python
import jax
import jax.numpy as jnp
from jax import lax
from jax.experimental import pallas as pl
from jax.experimental.pallas import tpu as pltpu
from jax.sharding import PartitionSpec as P

MESH = pl.DeviceIdType.MESH
HEADS = 12
HDIM = 128
NX, NZ, NC = 4, 8, 8
HPD = HEADS // NX
ROWS = 32
VROWS = 256
VBLK = 128
LMAX = 8
KEYS = LMAX * ROWS
WIN = 2 * NX * NZ
TILES = 2 * NX
MASKED = -1e30
BF16 = jnp.bfloat16


def dev(c, x, z):
    return {"grp": c, "seq": x * NZ + z}


def enter(c, x, z):
    barrier = pltpu.get_barrier_semaphore()

    def greet(*where):
        pl.semaphore_signal(barrier, inc=1, device_id=dev(*where), device_id_type=MESH)

    for r in range(1, NX):
        greet(c, (x + r) % NX, z)
    greet(c, x, (z + 1) % NZ)
    greet(c, x, (z + NZ - 1) % NZ)

    @pl.when(c > 0)
    def _():
        greet(c - 1, x, z)

    @pl.when(c < NC - 1)
    def _():
        greet(c + 1, x, z)

    inner = jnp.logical_and(c > 0, c < NC - 1)
    pl.semaphore_wait(barrier, NX - 1 + 2 + 1 + inner.astype(jnp.int32))


def remote(src, dst, sems, at, where):
    return pltpu.make_async_remote_copy(
        src_ref=src,
        dst_ref=dst,
        send_sem=sems[0].at[at],
        recv_sem=sems[1].at[at],
        device_id=dev(*where),
        device_id_type=MESH,
    )


def head_cols(x, h):
    return pl.ds(pl.multiple_of((x * HPD + h) * HDIM, HDIM), HDIM)


def nt(a, b):
    return lax.dot_general(a, b, (((1,), (1,)), ((), ())), preferred_element_type=jnp.float32)


def tn(a, b):
    return lax.dot_general(a, b, (((0,), (0,)), ((), ())), preferred_element_type=jnp.float32)


def nn(a, b):
    return lax.dot_general(a, b, (((1,), (0,)), ((), ())), preferred_element_type=jnp.float32)


def kernel(
    q, g, k, v, lists, out_q, out_k, out_v,
    kv0, kv1, kv2, qg0, qg1, qg2, dq0, dq1, dq2, part0, part1, part2, edge0, edge1, edge2,
    moving0, moving1, moving2, landed0, landed1, landed2, final0, final1, final2,
    pads, mine, lists_v, lists_s, runs,
    k_send, k_recv, i_send, i_recv, v_send, v_recv, r_send, r_recv, e_send, e_recv,
    q_send, q_recv, b_send, b_recv, s_send, s_recv, f_send, f_recv, own_k, own_v, own_q, own_f, own_i,
):
    c, s = lax.axis_index("grp"), lax.axis_index("seq")
    x, z = s // NZ, s % NZ
    enter(c, x, z)
    audio, video, outs = (k, v), (q, g), (out_k, out_v)
    kv, qg, dq = (kv0, kv1, kv2), (qg0, qg1, qg2), (dq0, dq1, dq2)
    part, edge = (part0, part1, part2), (edge0, edge1, edge2)
    moving, landed, final = (moving0, moving1, moving2), (landed0, landed1, landed2), (final0, final1, final2)
    above, below = jnp.minimum(c + 1, NC - 1), jnp.maximum(c - 1, 0)
    has_above, has_below = c < NC - 1, c > 0
    started, kept = [], []

    def go(copy):
        copy.start()
        started.append(copy)

    def peers():
        return [(r - 1, (x + r) % NX, (x - r + NX) % NX) for r in range(1, NX)]

    def audio_copy(h, w, r, to, came):
        return remote(audio[w].at[:, head_cols(to, h)], kv[h].at[w, 2 + came, z], (k_send, k_recv), (h, w, r), (c, to, z))

    def video_copy(h, w, r, to, came):
        return remote(video[w].at[:, head_cols(to, h)], qg[h].at[w, came], (v_send, v_recv), (h, w, r), (c, to, z))

    def own_audio(h, w):
        return pltpu.make_async_copy(audio[w].at[:, head_cols(x, h)], kv[h].at[w, 2 + x, z], own_k.at[h, w])

    def own_video(h, w):
        return pltpu.make_async_copy(video[w].at[:, head_cols(x, h)], qg[h].at[w, x], own_v.at[h, w])

    def list_copy(r, to, came):
        return remote(mine, lists_v.at[came], (i_send, i_recv), r, (c, to, z))

    def ring(h, w, d, step, at):
        panel = kv[h].at[w, pl.ds(2, NX), (z + at) % NZ]
        return remote(panel, panel, (r_send, r_recv), (h, w, d, step), (c, x, (z + 1 - 2 * d + NZ) % NZ))

    def spread(h, w, rel):
        zz = (z + rel) % NZ

        @pl.when(has_above)
        def _():
            remote(kv[h].at[w, pl.ds(4, 2), zz], kv[h].at[w, pl.ds(0, 2), zz], (e_send, e_recv), (h, w, 0), (above, x, z)).start()

        @pl.when(has_below)
        def _():
            remote(kv[h].at[w, pl.ds(2, 2), zz], kv[h].at[w, pl.ds(6, 2), zz], (e_send, e_recv), (h, w, 1), (below, x, z)).start()

    def spread_wait(h, w, sent):
        @pl.when(has_above)
        def _():
            up = remote(kv[h].at[w, pl.ds(4, 2)], kv[h].at[w, pl.ds(0, 2)], (e_send, e_recv), (h, w, 0), (above, x, z))
            down = remote(kv[h].at[w, pl.ds(2, 2)], kv[h].at[w, pl.ds(6, 2)], (e_send, e_recv), (h, w, 1), (above, x, z))
            up.wait_send() if sent else down.wait_recv()

        @pl.when(has_below)
        def _():
            up = remote(kv[h].at[w, pl.ds(4, 2)], kv[h].at[w, pl.ds(0, 2)], (e_send, e_recv), (h, w, 0), (below, x, z))
            down = remote(kv[h].at[w, pl.ds(2, 2)], kv[h].at[w, pl.ds(6, 2)], (e_send, e_recv), (h, w, 1), (below, x, z))
            down.wait_send() if sent else up.wait_recv()

    for h in range(HPD):
        for w in range(2):
            for peer in peers():
                go(audio_copy(h, w, *peer[:2], x))
            own_audio(h, w).start()
    mine[...] = jnp.zeros_like(mine)
    mine[0:2, 0:LMAX] = lists[...]
    for peer in peers():
        go(list_copy(*peer[:2], x))
    pltpu.make_async_copy(mine, lists_v.at[x], own_i.at[0]).start()

    for h in range(HPD):
        for w in range(2):
            own_audio(h, w).wait()
            for peer in peers():
                audio_copy(h, w, *peer).wait_recv()
            for d in range(2):
                go(ring(h, w, d, 0, 0))
            spread(h, w, 0)
        if h == 0:
            for w in range(2):
                for peer in peers():
                    go(video_copy(h, w, *peer[:2], x))
                own_video(h, w).start()
    pads[:, :, 0:LMAX] = jnp.zeros((TILES, 2, LMAX, ROWS, HDIM), jnp.float32)
    pads[:, :, 2 * LMAX : 3 * LMAX] = jnp.zeros((TILES, 2, LMAX, ROWS, HDIM), jnp.float32)
    for h in range(HPD):

        @pl.when(c == 0)
        def _():
            edge[h][:, 0] = jnp.zeros((2,) + edge[h].shape[2:], BF16)

        @pl.when(c == NC - 1)
        def _():
            edge[h][:, 1] = jnp.zeros((2,) + edge[h].shape[2:], BF16)

    for step in range(1, 5):
        for h in range(HPD):
            for w in range(2):
                for d in range(2):
                    if step == 4 and w != d:
                        continue
                    rel = step if d else -step
                    ring(h, w, d, step - 1, rel + NZ).wait_recv()
                    if step < 3 or (step == 3 and w == d):
                        go(ring(h, w, d, step, rel + NZ))
                    spread(h, w, rel + NZ)
        if step < HPD:
            for w in range(2):
                for peer in peers():
                    go(video_copy(step, w, *peer[:2], x))
                own_video(step, w).start()

    pltpu.make_async_copy(mine, lists_v.at[x], own_i.at[0]).wait()
    for peer in peers():
        list_copy(*peer).wait_recv()
    fetched = pltpu.make_async_copy(lists_v, lists_s, own_i.at[1])
    fetched.start()
    fetched.wait()
    for t in range(TILES):
        count = jnp.int32(0)
        for j in range(LMAX):
            count += (lists_s[t // 2, t % 2, j] >= 0).astype(jnp.int32)
        runs[0, t] = jnp.clip(lists_s[t // 2, t % 2, 0] - (c * NX * NZ - NX * NZ // 2), 0, WIN - 1)
        runs[1, t] = count

    scale = HDIM**-0.5
    key_at = lax.broadcasted_iota(jnp.int32, (KEYS, VBLK), 0)

    def tiles(h, low, high):
        def pair(xd, _):
            for b in range(2):
                t = xd * 2 + b
                first, count = runs[0, t], runs[1, t]
                blocks = [jnp.minimum(first + jnp.where(j < count, j, 0), WIN - 1) for j in range(LMAX)]
                kt = jnp.concatenate([kv[h][0, e >> 3, e & 7] for e in blocks], axis=0)
                vt = jnp.concatenate([kv[h][1, e >> 3, e & 7] for e in blocks], axis=0)
                qt, gt = qg[h][0, xd, b * VBLK : (b + 1) * VBLK], qg[h][1, xd, b * VBLK : (b + 1) * VBLK]
                scores = jnp.where(key_at < count * ROWS, nt(kt, qt) * scale, MASKED)
                raw = jnp.exp(scores - jnp.max(scores, axis=0, keepdims=True))
                weights = raw * (1.0 / jnp.sum(raw, axis=0, keepdims=True))
                grad_weights = nt(vt, gt)
                inner = jnp.sum(weights * grad_weights, axis=0, keepdims=True)
                grad_scores = (weights * (grad_weights - inner) * scale).astype(BF16)
                pads[t, 1, LMAX : 2 * LMAX] = nn(weights.astype(BF16), gt).reshape(LMAX, ROWS, HDIM)
                pads[t, 0, LMAX : 2 * LMAX] = nn(grad_scores, qt).reshape(LMAX, ROWS, HDIM)
                dq[h][xd, b * VBLK : (b + 1) * VBLK] = tn(grad_scores, kt).astype(BF16)
            return 0

        lax.fori_loop(low, high, pair, 0)

    def place(h):
        for w in range(2):
            for line in range(2 * NX):
                near = range(max(0, line - NX) * 2, min(NX, line + 1) * 2)
                total = None
                for t in near:
                    term = pads[t, w, pl.ds(jnp.clip(line * NZ - runs[0, t] + LMAX, 0, 2 * LMAX), LMAX)]
                    total = term if total is None else total + term
                part[h][w, line] = total.astype(BF16)

    def query_copy(h, r, to, mine_at):
        return remote(dq[h].at[to], out_q.at[:, head_cols(mine_at, h)], (q_send, q_recv), (h, r), (c, to, z))

    def own_query(h):
        return pltpu.make_async_copy(dq[h].at[x], out_q.at[:, head_cols(x, h)], own_q.at[h])

    def edge_copy(h, w, d):
        line, to = ((6, above), (0, below))[d]
        return remote(part[h].at[w, pl.ds(line, 2)], edge[h].at[w, d], (b_send, b_recv), (h, w, d), (to, x, z))

    def hand_out(h):
        for w in range(2):

            @pl.when(has_above)
            def _():
                edge_copy(h, w, 0).start()

            @pl.when(has_below)
            def _():
                edge_copy(h, w, 1).start()

        for peer in peers():
            go(query_copy(h, *peer[:2], x))
        own_query(h).start()

    def edges_in(h, w):
        @pl.when(has_above)
        def _():
            edge_copy(h, w, 1).wait_recv()

        @pl.when(has_below)
        def _():
            edge_copy(h, w, 0).wait_recv()

    def total(h, w, rel):
        zz = (z + rel + NZ) % NZ
        low = part[h][w, 2:4, zz].astype(jnp.float32) + edge[h][w, 0, :, zz].astype(jnp.float32)
        high = part[h][w, 4:6, zz].astype(jnp.float32) + edge[h][w, 1, :, zz].astype(jnp.float32)
        return jnp.concatenate([low, high], axis=0)

    def sum_ring(h, w, d, dist):
        at = (w, d, dist - 1)
        return remote(moving[h].at[at], landed[h].at[at], (s_send, s_recv), (h, *at), (c, x, (z + 1 - 2 * d + NZ) % NZ))

    def sums(h, dist):
        for w in range(2):
            if dist == 4:
                edges_in(h, w)
            for d in range(2):
                if dist == 4 and w != d:
                    continue
                value = total(h, w, -dist if d else dist)
                if dist < 3 or (dist == 3 and w == d):
                    sum_ring(h, w, d, dist + 1).wait_recv()
                    value = value + landed[h][w, d, dist].astype(jnp.float32)
                moving[h][w, d, dist - 1] = value.astype(BF16)
                go(sum_ring(h, w, d, dist))

    def final_copy(h, w, r, to, mine_at):
        return remote(final[h].at[w, to], outs[w].at[:, head_cols(mine_at, h)], (f_send, f_recv), (h, w, r), (c, to, z))

    def own_final(h, w):
        return pltpu.make_async_copy(final[h].at[w, x], outs[w].at[:, head_cols(x, h)], own_f.at[h, w])

    def finish(h):
        for w in range(2):
            value = total(h, w, 0)
            for d in range(2):
                sum_ring(h, w, d, 1).wait_recv()
                value = value + landed[h][w, d, 0].astype(jnp.float32)
            final[h][w] = value.astype(BF16)
            for peer in peers():
                go(final_copy(h, w, *peer[:2], x))
            own_final(h, w).start()

    def ready(h):
        for w in range(2):
            spread_wait(h, w, False)
            own_video(h, w).wait()
            for peer in peers():
                video_copy(h, w, *peer).wait_recv()

    def compute(h, between):
        ready(h)
        half = NX // 2
        tiles(h, 0, half)
        between[0]()
        tiles(h, half, NX)
        between[1]()
        place(h)
        hand_out(h)

    nothing = lambda: None
    compute(0, (nothing, nothing))
    compute(1, (nothing, lambda: sums(0, 4)))
    compute(2, (lambda: sums(0, 3), lambda: sums(0, 2)))
    sums(1, 4)
    sums(0, 1)
    sums(1, 3)
    sums(2, 4)
    finish(0)
    sums(1, 2)
    sums(2, 3)
    sums(1, 1)
    sums(2, 2)
    finish(1)
    sums(2, 1)
    finish(2)

    for h in range(HPD):
        own_query(h).wait()
        for peer in peers():
            r, to, came = peer
            query_copy(h, r, to, came).wait_recv()
        for w in range(2):
            spread_wait(h, w, True)
            own_final(h, w).wait()
            for r, to, came in peers():
                final_copy(h, w, r, to, came).wait_recv()

            @pl.when(has_above)
            def _():
                edge_copy(h, w, 0).wait_send()

            @pl.when(has_below)
            def _():
                edge_copy(h, w, 1).wait_send()

    for copy in started:
        copy.wait_send()


ANY = pl.BlockSpec(memory_space=pl.ANY)
VMEM = pl.BlockSpec(memory_space=pltpu.VMEM)


def sems(*shape):
    return [pltpu.SemaphoreType.DMA(shape)] * 2


def each(*shape):
    return [pltpu.VMEM(shape, BF16)] * HPD


def per_device(q, k, v, g, lists):
    return pl.pallas_call(
        kernel,
        out_shape=tuple(jax.ShapeDtypeStruct(a.shape, BF16) for a in (q, k, v)),
        in_specs=[ANY] * 4 + [VMEM],
        out_specs=(ANY,) * 3,
        scratch_shapes=[
            *each(2, 2 * NX, NZ, ROWS, HDIM),
            *each(2, NX, VROWS, HDIM),
            *each(NX, VROWS, HDIM),
            *each(2, 2 * NX, NZ, ROWS, HDIM),
            *each(2, 2, 2, NZ, ROWS, HDIM),
            *each(2, 2, 4, NX, ROWS, HDIM),
            *each(2, 2, 4, NX, ROWS, HDIM),
            *each(2, NX, ROWS, HDIM),
            pltpu.VMEM((TILES, 2, 3 * LMAX, ROWS, HDIM), jnp.float32),
            pltpu.VMEM((8, 128), jnp.int32),
            pltpu.VMEM((NX, 8, 128), jnp.int32),
            pltpu.SMEM((NX, 8, 128), jnp.int32),
            pltpu.SMEM((2, TILES), jnp.int32),
            *sems(HPD, 2, NX - 1), *sems(NX - 1), *sems(HPD, 2, NX - 1), *sems(HPD, 2, 2, 4), *sems(HPD, 2, 2),
            *sems(HPD, NX - 1), *sems(HPD, 2, 2), *sems(HPD, 2, 2, 4), *sems(HPD, 2, NX - 1),
            pltpu.SemaphoreType.DMA((HPD, 2)),
            pltpu.SemaphoreType.DMA((HPD, 2)),
            pltpu.SemaphoreType.DMA((HPD,)),
            pltpu.SemaphoreType.DMA((HPD, 2)),
            pltpu.SemaphoreType.DMA((2,)),
        ],
        compiler_params=pltpu.CompilerParams(
            collective_id=0, has_side_effects=True, vmem_limit_bytes=48 * 2**20
        ),
        name="cross_attention_backward",
    )(q, g, k, v, lists)


def solution(mesh):
    placed = P(("grp", "seq"), None)
    return jax.shard_map(
        per_device,
        mesh=mesh,
        in_specs=(placed,) * 5,
        out_specs=(placed,) * 3,
        check_vma=False,
    )
```

time: 713 us -> 79.7 us (0.11)
  waiting for transfers between devices: 555 us -> 0 us
  Pallas kernels: 0 us -> 71.2 us
  local copies, waits for them, and re-layouts: 72.9 us -> 6.88 us
  other arithmetic: 44.1 us -> 0 us
  matrix products: 17.6 us -> 0 us
  between operations: 14 us -> 0.65 us
  starting transfers between devices: 8.76 us -> 0 us
    reduce_scatter x2 -> x0, waiting for transfers between devices: 430 us -> none  [the longest x1 216 us: per_device(): lax.psum_scatter(rim_blocks.reshape(2, seq_count * audio_rows, model_widt...]
    all_gather x1 -> x0, waiting for transfers between devices: 93.8 us -> none  [per_device(): group_panel = lax.all_gather(stacked, 'seq', axis=1, tiled=True)]
    pallas_call x0 -> x1, Pallas kernels: none -> 71.2 us  [per_device(): pl.pallas_call(kernel, out_shape=tuple((jax.ShapeDtypeStruct(a.shape, BF1...]
    ppermute x4 -> x0, waiting for transfers between devices: 31.4 us -> none  [the longest x1 27.6 us: extended_2(): after = lax.ppermute(initial, axis, down)]
    dot_general x5 -> x0, matrix products: 17.6 us -> none  [the longest x1 8.05 us: block_grads(): jnp.einsum('bhrk,brhd->bkhd', grad_scores, query_heads, preferred_element...]
    scatter-add x1 -> x0, other arithmetic: 15.1 us -> none  [one_step(): accumulated = accumulated.at[:, flat_slots].add(contrib)]
    slice x4 -> x0, local copies, waits for them, and re-layouts: 14.3 us -> none  [the longest x1 6.13 us: per_device(): own_blocks = rounded[:, reach:reach + seq_count]]
    concatenate x2 -> x0, other arithmetic: 12.4 us -> none  [the longest x1 9.3 us: extended_2(): array = jnp.concatenate([before, array, after], axis=dim)]
  transfers between devices with their start and end apart: 7 -> 0, of which waited for: 5 -> 0; matrix products, arithmetic and copies ran while one was open for 3% -> 0% of each run, Pallas kernels for 0% -> 0%
where the time goes in v2:
time: 79.7 us; the launch traced here: 78.7 us
  Pallas kernels  71.2 us (89%)
  local copies, waits for them, and re-layouts  6.88 us (9%)
    pallas_call x1, Pallas kernels, per_device(): pl.pallas_call(kernel, out_shape=tuple((jax.ShapeDtypeStruct(a.shape, BF1...  71.2 us
    unnamed x13, local copies, waits for them, and re-layouts  6.88 us

profile of v2, /device:TPU:8, one launch (start us, length us, event | category | flops | bytes accessed | tf_op | source)
XLA Modules:
  0.0 78.7 jit_solution(6698196557726550906)
XLA Ops:
  0.6 0.0 copy-start
  0.6 1.1 %copy-done = bf16[256,1536]{1,0:T(8,128)(2,1)S(1)} copy-done((bf16[256,1536]{1,0:T(8,128)(2,1)S(1)}, bf16[256,1536]{1,0:T(8,128)(2,1)}, u32[]{:S(2)}) %copy-start) | copy-done | bytes 786456
  1.8 0.0 copy-start.1
  1.8 1.1 %copy-done.1 = bf16[256,1536]{1,0:T(8,128)(2,1)S(1)} copy-done((bf16[256,1536]{1,0:T(8,128)(2,1)S(1)}, bf16[256,1536]{1,0:T(8,128)(2,1)}, u32[]{:S(2)}) %copy-start.1) | copy-done | bytes 786456
  2.9 0.0 copy-start.2
  2.9 0.9 %copy-done.2 = bf16[32,1536]{1,0:T(8,128)(2,1)S(1)} copy-done((bf16[32,1536]{1,0:T(8,128)(2,1)S(1)}, bf16[32,1536]{1,0:T(8,128)(2,1)}, u32[]{:S(2)}) %copy-start.2) | copy-done | bytes 98328
  3.8 0.0 copy-start.3
  3.8 0.9 %copy-done.3 = bf16[32,1536]{1,0:T(8,128)(2,1)S(1)} copy-done((bf16[32,1536]{1,0:T(8,128)(2,1)S(1)}, bf16[32,1536]{1,0:T(8,128)(2,1)}, u32[]{:S(2)}) %copy-start.3) | copy-done | bytes 98328
  4.7 0.0 copy-start.4
  4.7 0.7 copy-done.4
  5.4 71.2 %cross_attention_backward.1 = (bf16[256,1536]{1,0:T(8,128)(2,1)S(1)}, bf16[32,1536]{1,0:T(8,128)(2,1)S(1)}, bf16[32,1536]{1,0:T(8,128)(2,1)S(1)}) custom-call(bf16[256,1536]{1,0:T(8,128)(2,1)S(1)} %copy-done, bf16[256,1536]{1,0:T(8,128)(2,1)S(1)} %copy-done.1, bf16[32,1536]{1,0:T(8,128)(2,1)S(1)} %copy-done.2, bf16[32,1536]{1,0:T(8,128)(2,1)S(1)} %copy-done.3, ...), custom_call_target="tpu_custom_call" | custom-call | tf_op jit(solution)/shard_map/cross_attention_backward/pallas_call | solution.py:393
  76.5 0.9 %copy.11 = bf16[256,1536]{1,0:T(8,128)(2,1)} copy(bf16[256,1536]{1,0:T(8,128)(2,1)S(1)} %get-tuple-element.6) | data formatting | bytes 1572864
  77.4 0.6 copy.12
  78.1 0.6 copy.13
Async XLA Ops:
  0.6 1.1 %copy-start = (bf16[256,1536]{1,0:T(8,128)(2,1)S(1)}, bf16[256,1536]{1,0:T(8,128)(2,1)}, u32[]{:S(2)}) copy-start(bf16[256,1536]{1,0:T(8,128)(2,1)} %q.1) | copy-start | bytes 2359300
  1.8 1.1 %copy-start.1 = (bf16[256,1536]{1,0:T(8,128)(2,1)S(1)}, bf16[256,1536]{1,0:T(8,128)(2,1)}, u32[]{:S(2)}) copy-start(bf16[256,1536]{1,0:T(8,128)(2,1)} %g.1) | copy-start | bytes 2359300
  2.9 0.9 %copy-start.2 = (bf16[32,1536]{1,0:T(8,128)(2,1)S(1)}, bf16[32,1536]{1,0:T(8,128)(2,1)}, u32[]{:S(2)}) copy-start(bf16[32,1536]{1,0:T(8,128)(2,1)} %k.1) | copy-start | bytes 294916
  3.8 0.9 %copy-start.3 = (bf16[32,1536]{1,0:T(8,128)(2,1)S(1)}, bf16[32,1536]{1,0:T(8,128)(2,1)}, u32[]{:S(2)}) copy-start(bf16[32,1536]{1,0:T(8,128)(2,1)} %v.1) | copy-start | bytes 294916
  4.7 0.7 copy-start.4

commit v3 on v2

--- a/solution.py
+++ b/solution.py
@@ -17,7 +17,10 @@
 KEYS = LMAX * ROWS
 WIN = 2 * NX * NZ
 TILES = 2 * NX
+SPREADS = ((0, 5), (5, 2), (7, 1))
+EDGES = ((5, 3), (0, 5))
 MASKED = -1e30
+LOG2E = 1.4426950408889634
 BF16 = jnp.bfloat16
 
 
@@ -57,6 +60,10 @@
         device_id=dev(*where),
         device_id_type=MESH,
     )
+
+
+def at(rel):
+    return NZ - 1 if abs(rel) == 4 else 2 * rel if rel >= 0 else -2 * rel - 1
 
 
 def head_cols(x, h):
@@ -102,13 +109,13 @@
         return [(r - 1, (x + r) % NX, (x - r + NX) % NX) for r in range(1, NX)]
 
     def audio_copy(h, w, r, to, came):
-        return remote(audio[w].at[:, head_cols(to, h)], kv[h].at[w, 2 + came, z], (k_send, k_recv), (h, w, r), (c, to, z))
+        return remote(audio[w].at[:, head_cols(to, h)], kv[h].at[w, 2 + came, 0], (k_send, k_recv), (h, w, r), (c, to, z))
 
     def video_copy(h, w, r, to, came):
         return remote(video[w].at[:, head_cols(to, h)], qg[h].at[w, came], (v_send, v_recv), (h, w, r), (c, to, z))
 
     def own_audio(h, w):
-        return pltpu.make_async_copy(audio[w].at[:, head_cols(x, h)], kv[h].at[w, 2 + x, z], own_k.at[h, w])
+        return pltpu.make_async_copy(audio[w].at[:, head_cols(x, h)], kv[h].at[w, 2 + x, 0], own_k.at[h, w])
 
     def own_video(h, w):
         return pltpu.make_async_copy(video[w].at[:, head_cols(x, h)], qg[h].at[w, x], own_v.at[h, w])
@@ -116,33 +123,38 @@
     def list_copy(r, to, came):
         return remote(mine, lists_v.at[came], (i_send, i_recv), r, (c, to, z))
 
-    def ring(h, w, d, step, at):
-        panel = kv[h].at[w, pl.ds(2, NX), (z + at) % NZ]
-        return remote(panel, panel, (r_send, r_recv), (h, w, d, step), (c, x, (z + 1 - 2 * d + NZ) % NZ))
-
-    def spread(h, w, rel):
-        zz = (z + rel) % NZ
-
+    def ring(h, w, d, step):
+        sign = 1 - 2 * d
+        source = kv[h].at[w, pl.ds(2, NX), at(-sign * step)]
+        target = kv[h].at[w, pl.ds(2, NX), at(-sign * (step + 1))]
+        return remote(source, target, (r_send, r_recv), (h, w, d, step), (c, x, (z + sign + NZ) % NZ))
+
+    def spread_copy(h, w, d, part_of):
+        low, count = SPREADS[part_of]
+        span = pl.ds(low, count)
+        line, there, to = ((4, 0, above), (2, 6, below))[d]
+        source, target = kv[h].at[w, pl.ds(line, 2), span], kv[h].at[w, pl.ds(there, 2), span]
+        return remote(source, target, (e_send, e_recv), (h, w, d, part_of), (to, x, z))
+
+    def spread(h, w, part_of):
         @pl.when(has_above)
         def _():
-            remote(kv[h].at[w, pl.ds(4, 2), zz], kv[h].at[w, pl.ds(0, 2), zz], (e_send, e_recv), (h, w, 0), (above, x, z)).start()
+            spread_copy(h, w, 0, part_of).start()
 
         @pl.when(has_below)
         def _():
-            remote(kv[h].at[w, pl.ds(2, 2), zz], kv[h].at[w, pl.ds(6, 2), zz], (e_send, e_recv), (h, w, 1), (below, x, z)).start()
+            spread_copy(h, w, 1, part_of).start()
 
     def spread_wait(h, w, sent):
-        @pl.when(has_above)
-        def _():
-            up = remote(kv[h].at[w, pl.ds(4, 2)], kv[h].at[w, pl.ds(0, 2)], (e_send, e_recv), (h, w, 0), (above, x, z))
-            down = remote(kv[h].at[w, pl.ds(2, 2)], kv[h].at[w, pl.ds(6, 2)], (e_send, e_recv), (h, w, 1), (above, x, z))
-            up.wait_send() if sent else down.wait_recv()
-
-        @pl.when(has_below)
-        def _():
-            up = remote(kv[h].at[w, pl.ds(4, 2)], kv[h].at[w, pl.ds(0, 2)], (e_send, e_recv), (h, w, 0), (below, x, z))
-            down = remote(kv[h].at[w, pl.ds(2, 2)], kv[h].at[w, pl.ds(6, 2)], (e_send, e_recv), (h, w, 1), (below, x, z))
-            down.wait_send() if sent else up.wait_recv()
+        for part_of in range(len(SPREADS)):
+
+            @pl.when(has_above)
+            def _():
+                spread_copy(h, w, 0, part_of).wait_send() if sent else spread_copy(h, w, 1, part_of).wait_recv()
+
+            @pl.when(has_below)
+            def _():
+                spread_copy(h, w, 1, part_of).wait_send() if sent else spread_copy(h, w, 0, part_of).wait_recv()
 
     for h in range(HPD):
         for w in range(2):
@@ -161,8 +173,7 @@
             for peer in peers():
                 audio_copy(h, w, *peer).wait_recv()
             for d in range(2):
-                go(ring(h, w, d, 0, 0))
-            spread(h, w, 0)
+                go(ring(h, w, d, 0))
         if h == 0:
             for w in range(2):
                 for peer in peers():
@@ -186,11 +197,11 @@
                 for d in range(2):
                     if step == 4 and w != d:
                         continue
-                    rel = step if d else -step
-                    ring(h, w, d, step - 1, rel + NZ).wait_recv()
+                    ring(h, w, d, step - 1).wait_recv()
                     if step < 3 or (step == 3 and w == d):
-                        go(ring(h, w, d, step, rel + NZ))
-                    spread(h, w, rel + NZ)
+                        go(ring(h, w, d, step))
+                if step > 1:
+                    spread(h, w, step - 2)
         if step < HPD:
             for w in range(2):
                 for peer in peers():
@@ -211,29 +222,32 @@
         runs[1, t] = count
 
     scale = HDIM**-0.5
-    key_at = lax.broadcasted_iota(jnp.int32, (KEYS, VBLK), 0)
-
-    def tiles(h, low, high):
-        def pair(xd, _):
-            for b in range(2):
-                t = xd * 2 + b
-                first, count = runs[0, t], runs[1, t]
-                blocks = [jnp.minimum(first + jnp.where(j < count, j, 0), WIN - 1) for j in range(LMAX)]
-                kt = jnp.concatenate([kv[h][0, e >> 3, e & 7] for e in blocks], axis=0)
-                vt = jnp.concatenate([kv[h][1, e >> 3, e & 7] for e in blocks], axis=0)
-                qt, gt = qg[h][0, xd, b * VBLK : (b + 1) * VBLK], qg[h][1, xd, b * VBLK : (b + 1) * VBLK]
-                scores = jnp.where(key_at < count * ROWS, nt(kt, qt) * scale, MASKED)
-                raw = jnp.exp(scores - jnp.max(scores, axis=0, keepdims=True))
-                weights = raw * (1.0 / jnp.sum(raw, axis=0, keepdims=True))
-                grad_weights = nt(vt, gt)
-                inner = jnp.sum(weights * grad_weights, axis=0, keepdims=True)
-                grad_scores = (weights * (grad_weights - inner) * scale).astype(BF16)
-                pads[t, 1, LMAX : 2 * LMAX] = nn(weights.astype(BF16), gt).reshape(LMAX, ROWS, HDIM)
-                pads[t, 0, LMAX : 2 * LMAX] = nn(grad_scores, qt).reshape(LMAX, ROWS, HDIM)
-                dq[h][xd, b * VBLK : (b + 1) * VBLK] = tn(grad_scores, kt).astype(BF16)
-            return 0
-
-        lax.fori_loop(low, high, pair, 0)
+
+    def tiles(h):
+        loaded, ready_terms = [], []
+        for t in range(TILES):
+            first, count = runs[0, t], runs[1, t]
+            blocks = [jnp.minimum(first + jnp.where(j < count, j, 0), WIN - 1) for j in range(LMAX)]
+            places = [(e >> 3, ((e & 7) - z + NZ) & 7) for e in blocks]
+            places = [(line, jnp.where(rel < 4, 2 * rel, 15 - 2 * rel)) for line, rel in places]
+            kt = jnp.concatenate([kv[h][0, line, where] for line, where in places], axis=0)
+            vt = jnp.concatenate([kv[h][1, line, where] for line, where in places], axis=0)
+            rows = pl.ds(t % 2 * VBLK, VBLK)
+            qt, gt = qg[h][0, t // 2, rows], qg[h][1, t // 2, rows]
+            loaded.append((count, kt, qt, gt, nt(kt, qt), nt(vt, gt)))
+        for count, kt, qt, gt, products, grad_weights in loaded:
+            dead = [jnp.full((ROWS, VBLK), jnp.where(j < count, 0.0, MASKED), jnp.float32) for j in range(LMAX)]
+            scores = products * (scale * LOG2E) + jnp.concatenate(dead, axis=0)
+            raw = jnp.exp2(scores - jnp.max(scores, axis=0, keepdims=True))
+            inverse = 1.0 / jnp.sum(raw, axis=0, keepdims=True)
+            inner = jnp.sum(raw * grad_weights, axis=0, keepdims=True) * inverse
+            weights_low = (raw * inverse).astype(BF16)
+            grad_scores = (raw * ((grad_weights - inner) * (inverse * scale))).astype(BF16)
+            ready_terms.append((kt, qt, gt, weights_low, grad_scores))
+        for t, (kt, qt, gt, weights_low, grad_scores) in enumerate(ready_terms):
+            pads[t, 1, LMAX : 2 * LMAX] = nn(weights_low, gt).reshape(LMAX, ROWS, HDIM)
+            pads[t, 0, LMAX : 2 * LMAX] = nn(grad_scores, qt).reshape(LMAX, ROWS, HDIM)
+            dq[h][t // 2, pl.ds(t % 2 * VBLK, VBLK)] = tn(grad_scores, kt).astype(BF16)
 
     def place(h):
         for w in range(2):
@@ -243,7 +257,10 @@
                 for t in near:
                     term = pads[t, w, pl.ds(jnp.clip(line * NZ - runs[0, t] + LMAX, 0, 2 * LMAX), LMAX)]
                     total = term if total is None else total + term
-                part[h][w, line] = total.astype(BF16)
+                total = total.astype(BF16)
+                for zz in range(NZ):
+                    rel = (zz - z + NZ) & 7
+                    part[h][w, line, jnp.where(rel < 4, 2 * rel, 15 - 2 * rel)] = total[zz]
 
     def query_copy(h, r, to, mine_at):
         return remote(dq[h].at[to], out_q.at[:, head_cols(mine_at, h)], (q_send, q_recv), (h, r), (c, to, z))
@@ -251,48 +268,51 @@
     def own_query(h):
         return pltpu.make_async_copy(dq[h].at[x], out_q.at[:, head_cols(x, h)], own_q.at[h])
 
-    def edge_copy(h, w, d):
+    def edge_copy(h, w, d, part_of):
+        low, count = EDGES[part_of]
         line, to = ((6, above), (0, below))[d]
-        return remote(part[h].at[w, pl.ds(line, 2)], edge[h].at[w, d], (b_send, b_recv), (h, w, d), (to, x, z))
+        source, target = part[h].at[w, pl.ds(line, 2), pl.ds(low, count)], edge[h].at[w, d, :, pl.ds(low, count)]
+        return remote(source, target, (b_send, b_recv), (h, w, d, part_of), (to, x, z))
 
     def hand_out(h):
-        for w in range(2):
-
-            @pl.when(has_above)
-            def _():
-                edge_copy(h, w, 0).start()
-
-            @pl.when(has_below)
-            def _():
-                edge_copy(h, w, 1).start()
+        for part_of in range(len(EDGES)):
+            for w in range(2):
+
+                @pl.when(has_above)
+                def _():
+                    edge_copy(h, w, 0, part_of).start()
+
+                @pl.when(has_below)
+                def _():
+                    edge_copy(h, w, 1, part_of).start()
 
         for peer in peers():
             go(query_copy(h, *peer[:2], x))
         own_query(h).start()
 
-    def edges_in(h, w):
+    def edges_in(h, w, part_of):
         @pl.when(has_above)
         def _():
-            edge_copy(h, w, 1).wait_recv()
+            edge_copy(h, w, 1, part_of).wait_recv()
 
         @pl.when(has_below)
         def _():
-            edge_copy(h, w, 0).wait_recv()
+            edge_copy(h, w, 0, part_of).wait_recv()
 
     def total(h, w, rel):
-        zz = (z + rel + NZ) % NZ
-        low = part[h][w, 2:4, zz].astype(jnp.float32) + edge[h][w, 0, :, zz].astype(jnp.float32)
-        high = part[h][w, 4:6, zz].astype(jnp.float32) + edge[h][w, 1, :, zz].astype(jnp.float32)
+        p = at(rel)
+        low = part[h][w, 2:4, p].astype(jnp.float32) + edge[h][w, 0, :, p].astype(jnp.float32)
+        high = part[h][w, 4:6, p].astype(jnp.float32) + edge[h][w, 1, :, p].astype(jnp.float32)
         return jnp.concatenate([low, high], axis=0)
 
     def sum_ring(h, w, d, dist):
-        at = (w, d, dist - 1)
-        return remote(moving[h].at[at], landed[h].at[at], (s_send, s_recv), (h, *at), (c, x, (z + 1 - 2 * d + NZ) % NZ))
+        slot = (w, d, dist - 1)
+        return remote(moving[h].at[slot], landed[h].at[slot], (s_send, s_recv), (h, *slot), (c, x, (z + 1 - 2 * d + NZ) % NZ))
 
     def sums(h, dist):
         for w in range(2):
-            if dist == 4:
-                edges_in(h, w)
+            if dist in (4, 2):
+                edges_in(h, w, 0 if dist == 4 else 1)
             for d in range(2):
                 if dist == 4 and w != d:
                     continue
@@ -327,32 +347,23 @@
             for peer in peers():
                 video_copy(h, w, *peer).wait_recv()
 
-    def compute(h, between):
+    def compute(h):
         ready(h)
-        half = NX // 2
-        tiles(h, 0, half)
-        between[0]()
-        tiles(h, half, NX)
-        between[1]()
+        tiles(h)
         place(h)
         hand_out(h)
 
-    nothing = lambda: None
-    compute(0, (nothing, nothing))
-    compute(1, (nothing, lambda: sums(0, 4)))
-    compute(2, (lambda: sums(0, 3), lambda: sums(0, 2)))
+    compute(0)
+    compute(1)
+    sums(0, 4)
+    compute(2)
     sums(1, 4)
-    sums(0, 1)
-    sums(1, 3)
     sums(2, 4)
-    finish(0)
-    sums(1, 2)
-    sums(2, 3)
-    sums(1, 1)
-    sums(2, 2)
-    finish(1)
-    sums(2, 1)
-    finish(2)
+    for dist in (3, 2, 1):
+        for h in range(HPD):
+            sums(h, dist)
+    for h in range(HPD):
+        finish(h)
 
     for h in range(HPD):
         own_query(h).wait()
@@ -365,19 +376,21 @@
             for r, to, came in peers():
                 final_copy(h, w, r, to, came).wait_recv()
 
-            @pl.when(has_above)
-            def _():
-                edge_copy(h, w, 0).wait_send()
-
-            @pl.when(has_below)
-            def _():
-                edge_copy(h, w, 1).wait_send()
+            for part_of in range(len(EDGES)):
+
+                @pl.when(has_above)
+                def _():
+                    edge_copy(h, w, 0, part_of).wait_send()
+
+                @pl.when(has_below)
+                def _():
+                    edge_copy(h, w, 1, part_of).wait_send()
 
     for copy in started:
         copy.wait_send()
 
 
-ANY = pl.BlockSpec(memory_space=pl.ANY)
+HBM = pl.BlockSpec(memory_space=pltpu.HBM)
 VMEM = pl.BlockSpec(memory_space=pltpu.VMEM)
 
 
@@ -393,8 +406,8 @@
     return pl.pallas_call(
         kernel,
         out_shape=tuple(jax.ShapeDtypeStruct(a.shape, BF16) for a in (q, k, v)),
-        in_specs=[ANY] * 4 + [VMEM],
-        out_specs=(ANY,) * 3,
+        in_specs=[HBM] * 4 + [VMEM],
+        out_specs=(HBM,) * 3,
         scratch_shapes=[
             *each(2, 2 * NX, NZ, ROWS, HDIM),
             *each(2, NX, VROWS, HDIM),
@@ -409,8 +422,8 @@
             pltpu.VMEM((NX, 8, 128), jnp.int32),
             pltpu.SMEM((NX, 8, 128), jnp.int32),
             pltpu.SMEM((2, TILES), jnp.int32),
-            *sems(HPD, 2, NX - 1), *sems(NX - 1), *sems(HPD, 2, NX - 1), *sems(HPD, 2, 2, 4), *sems(HPD, 2, 2),
-            *sems(HPD, NX - 1), *sems(HPD, 2, 2), *sems(HPD, 2, 2, 4), *sems(HPD, 2, NX - 1),
+            *sems(HPD, 2, NX - 1), *sems(NX - 1), *sems(HPD, 2, NX - 1), *sems(HPD, 2, 2, 4), *sems(HPD, 2, 2, len(SPREADS)),
+            *sems(HPD, NX - 1), *sems(HPD, 2, 2, len(EDGES)), *sems(HPD, 2, 2, 4), *sems(HPD, 2, NX - 1),
             pltpu.SemaphoreType.DMA((HPD, 2)),
             pltpu.SemaphoreType.DMA((HPD, 2)),
             pltpu.SemaphoreType.DMA((HPD,)),

time: 79.7 us -> 71.6 us (0.90)
  Pallas kernels: 71.2 us -> 63.5 us
    pallas_call x1, Pallas kernels: 71.2 us -> 63.5 us  [per_device(): pl.pallas_call(kernel, out_shape=tuple((jax.ShapeDtypeStruct(a.shape, BF1...]
where the time goes in v3:
time: 71.6 us; the launch traced here: 71.1 us
  Pallas kernels  63.5 us (89%)
  local copies, waits for them, and re-layouts  6.88 us (10%)
    pallas_call x1, Pallas kernels, per_device(): pl.pallas_call(kernel, out_shape=tuple((jax.ShapeDtypeStruct(a.shape, BF1...  63.5 us
    unnamed x13, local copies, waits for them, and re-layouts  6.88 us

profile of v3, /device:TPU:8, one launch (start us, length us, event | category | flops | bytes accessed | tf_op | source)
XLA Modules:
  0.0 71.1 jit_solution(635534673544446114)
XLA Ops:
  0.6 0.0 copy-start
  0.6 1.1 %copy-done = bf16[256,1536]{1,0:T(8,128)(2,1)S(1)} copy-done((bf16[256,1536]{1,0:T(8,128)(2,1)S(1)}, bf16[256,1536]{1,0:T(8,128)(2,1)}, u32[]{:S(2)}) %copy-start) | copy-done | bytes 786456
  1.8 0.0 copy-start.1
  1.8 1.1 %copy-done.1 = bf16[256,1536]{1,0:T(8,128)(2,1)S(1)} copy-done((bf16[256,1536]{1,0:T(8,128)(2,1)S(1)}, bf16[256,1536]{1,0:T(8,128)(2,1)}, u32[]{:S(2)}) %copy-start.1) | copy-done | bytes 786456
  2.9 0.0 copy-start.2
  2.9 0.9 %copy-done.2 = bf16[32,1536]{1,0:T(8,128)(2,1)S(1)} copy-done((bf16[32,1536]{1,0:T(8,128)(2,1)S(1)}, bf16[32,1536]{1,0:T(8,128)(2,1)}, u32[]{:S(2)}) %copy-start.2) | copy-done | bytes 98328
  3.8 0.0 copy-start.3
  3.8 0.9 %copy-done.3 = bf16[32,1536]{1,0:T(8,128)(2,1)S(1)} copy-done((bf16[32,1536]{1,0:T(8,128)(2,1)S(1)}, bf16[32,1536]{1,0:T(8,128)(2,1)}, u32[]{:S(2)}) %copy-start.3) | copy-done | bytes 98328
  4.7 0.0 copy-start.4
  4.7 0.7 copy-done.4
  5.4 63.5 %cross_attention_backward.1 = (bf16[256,1536]{1,0:T(8,128)(2,1)S(1)}, bf16[32,1536]{1,0:T(8,128)(2,1)S(1)}, bf16[32,1536]{1,0:T(8,128)(2,1)S(1)}) custom-call(bf16[256,1536]{1,0:T(8,128)(2,1)S(1)} %copy-done, bf16[256,1536]{1,0:T(8,128)(2,1)S(1)} %copy-done.1, bf16[32,1536]{1,0:T(8,128)(2,1)S(1)} %copy-done.2, bf16[32,1536]{1,0:T(8,128)(2,1)S(1)} %copy-done.3, ...), custom_call_target="tpu_custom_call" | custom-call | tf_op jit(solution)/shard_map/cross_attention_backward/pallas_call | solution.py:406
  68.9 0.9 %copy.11 = bf16[256,1536]{1,0:T(8,128)(2,1)} copy(bf16[256,1536]{1,0:T(8,128)(2,1)S(1)} %get-tuple-element.6) | data formatting | bytes 1572864
  69.8 0.6 copy.12
  70.4 0.6 copy.13
Async XLA Ops:
  0.6 1.1 %copy-start = (bf16[256,1536]{1,0:T(8,128)(2,1)S(1)}, bf16[256,1536]{1,0:T(8,128)(2,1)}, u32[]{:S(2)}) copy-start(bf16[256,1536]{1,0:T(8,128)(2,1)} %q.1) | copy-start | bytes 2359300
  1.8 1.1 %copy-start.1 = (bf16[256,1536]{1,0:T(8,128)(2,1)S(1)}, bf16[256,1536]{1,0:T(8,128)(2,1)}, u32[]{:S(2)}) copy-start(bf16[256,1536]{1,0:T(8,128)(2,1)} %g.1) | copy-start | bytes 2359300
  2.9 0.9 %copy-start.2 = (bf16[32,1536]{1,0:T(8,128)(2,1)S(1)}, bf16[32,1536]{1,0:T(8,128)(2,1)}, u32[]{:S(2)}) copy-start(bf16[32,1536]{1,0:T(8,128)(2,1)} %k.1) | copy-start | bytes 294916
  3.8 0.9 %copy-start.3 = (bf16[32,1536]{1,0:T(8,128)(2,1)S(1)}, bf16[32,1536]{1,0:T(8,128)(2,1)}, u32[]{:S(2)}) copy-start(bf16[32,1536]{1,0:T(8,128)(2,1)} %v.1) | copy-start | bytes 294916
  4.7 0.7 copy-start.4

commit v4 on v3

--- a/solution.py
+++ b/solution.py
@@ -17,6 +17,8 @@
 KEYS = LMAX * ROWS
 WIN = 2 * NX * NZ
 TILES = 2 * NX
+REACH = 2
+EARLY, LATE = 0, HPD - 1
 SPREADS = ((0, 5), (5, 2), (7, 1))
 EDGES = ((5, 3), (0, 5))
 MASKED = -1e30
@@ -34,10 +36,10 @@
     def greet(*where):
         pl.semaphore_signal(barrier, inc=1, device_id=dev(*where), device_id_type=MESH)
 
-    for r in range(1, NX):
-        greet(c, (x + r) % NX, z)
-    greet(c, x, (z + 1) % NZ)
-    greet(c, x, (z + NZ - 1) % NZ)
+    for dz in range(-REACH, REACH + 1):
+        for r in range(NX):
+            if dz or r:
+                greet(c, (x + r) % NX, (z + dz + NZ) % NZ)
 
     @pl.when(c > 0)
     def _():
@@ -48,7 +50,7 @@
         greet(c + 1, x, z)
 
     inner = jnp.logical_and(c > 0, c < NC - 1)
-    pl.semaphore_wait(barrier, NX - 1 + 2 + 1 + inner.astype(jnp.int32))
+    pl.semaphore_wait(barrier, NX * (2 * REACH + 1) - 1 + 1 + inner.astype(jnp.int32))
 
 
 def remote(src, dst, sems, at, where):
@@ -86,9 +88,9 @@
     q, g, k, v, lists, out_q, out_k, out_v,
     kv0, kv1, kv2, qg0, qg1, qg2, dq0, dq1, dq2, part0, part1, part2, edge0, edge1, edge2,
     moving0, moving1, moving2, landed0, landed1, landed2, final0, final1, final2,
-    pads, mine, lists_v, lists_s, runs,
+    pads, mine, lists_v, lists_s, runs, leaving, home,
     k_send, k_recv, i_send, i_recv, v_send, v_recv, r_send, r_recv, e_send, e_recv,
-    q_send, q_recv, b_send, b_recv, s_send, s_recv, f_send, f_recv, own_k, own_v, own_q, own_f, own_i,
+    q_send, q_recv, b_send, b_recv, s_send, s_recv, f_send, f_recv, n_send, n_recv, h_send, h_recv, own_k, own_v, own_q, own_f, own_i,
 ):
     c, s = lax.axis_index("grp"), lax.axis_index("seq")
     x, z = s // NZ, s % NZ
@@ -156,7 +158,27 @@
             def _():
                 spread_copy(h, w, 1, part_of).wait_send() if sent else spread_copy(h, w, 0, part_of).wait_recv()
 
-    for h in range(HPD):
+    def near_copy(w, dz, r, to, came):
+        target = kv[EARLY].at[w, 2 + came, at(-dz)]
+        where = (c, to, (z + dz + NZ) % NZ)
+        return remote(audio[w].at[:, head_cols(to, EARLY)], target, (n_send, n_recv), (w, at(dz), r), where)
+
+    def near_peers(dz):
+        return [(r, (x + r) % NX, (x - r + NX) % NX) for r in range(NX) if dz or r]
+
+    def relay(w, d, far):
+        sign = 1 - 2 * d
+        hops = 2 if far else 1
+        source = kv[EARLY].at[w, pl.ds(2, NX), at(-sign * 2)]
+        target = kv[EARLY].at[w, pl.ds(2, NX), at(-sign * (2 + hops))]
+        return remote(source, target, (r_send, r_recv), (EARLY, w, d, hops), (c, x, (z + sign * hops + NZ) % NZ))
+
+    for w in range(2):
+        for dz in (2, -2, 1, -1, 0):
+            for r, to, _ in near_peers(dz):
+                go(near_copy(w, dz, r, to, x))
+        own_audio(EARLY, w).start()
+    for h in range(1, HPD):
         for w in range(2):
             for peer in peers():
                 go(audio_copy(h, w, *peer[:2], x))
@@ -167,46 +189,70 @@
         go(list_copy(*peer[:2], x))
     pltpu.make_async_copy(mine, lists_v.at[x], own_i.at[0]).start()
 
+    def send_video(h):
+        for w in range(2):
+            for peer in peers():
+                go(video_copy(h, w, *peer[:2], x))
+            own_video(h, w).start()
+
+    send_video(EARLY)
+    pads[:, :, 0:LMAX] = jnp.zeros((TILES, 2, LMAX, ROWS, HDIM), jnp.float32)
+    pads[:, :, 2 * LMAX : 3 * LMAX] = jnp.zeros((TILES, 2, LMAX, ROWS, HDIM), jnp.float32)
     for h in range(HPD):
+
+        @pl.when(c == 0)
+        def _():
+            edge[h][:, 0] = jnp.zeros((2,) + edge[h].shape[2:], BF16)
+
+        @pl.when(c == NC - 1)
+        def _():
+            edge[h][:, 1] = jnp.zeros((2,) + edge[h].shape[2:], BF16)
+
+    def near_in(w, dz):
+        for r, to, came in near_peers(dz):
+            near_copy(w, dz, r, to, came).wait_recv()
+
+    def first_step(h):
         for w in range(2):
             own_audio(h, w).wait()
             for peer in peers():
                 audio_copy(h, w, *peer).wait_recv()
             for d in range(2):
                 go(ring(h, w, d, 0))
-        if h == 0:
-            for w in range(2):
-                for peer in peers():
-                    go(video_copy(h, w, *peer[:2], x))
-                own_video(h, w).start()
-    pads[:, :, 0:LMAX] = jnp.zeros((TILES, 2, LMAX, ROWS, HDIM), jnp.float32)
-    pads[:, :, 2 * LMAX : 3 * LMAX] = jnp.zeros((TILES, 2, LMAX, ROWS, HDIM), jnp.float32)
-    for h in range(HPD):
-
-        @pl.when(c == 0)
-        def _():
-            edge[h][:, 0] = jnp.zeros((2,) + edge[h].shape[2:], BF16)
-
-        @pl.when(c == NC - 1)
-        def _():
-            edge[h][:, 1] = jnp.zeros((2,) + edge[h].shape[2:], BF16)
-
-    for step in range(1, 5):
-        for h in range(HPD):
-            for w in range(2):
-                for d in range(2):
-                    if step == 4 and w != d:
-                        continue
-                    ring(h, w, d, step - 1).wait_recv()
-                    if step < 3 or (step == 3 and w == d):
-                        go(ring(h, w, d, step))
-                if step > 1:
-                    spread(h, w, step - 2)
-        if step < HPD:
-            for w in range(2):
-                for peer in peers():
-                    go(video_copy(step, w, *peer[:2], x))
-                own_video(step, w).start()
+
+    def next_step(h, step):
+        for w in range(2):
+            for d in range(2):
+                if step == 4 and w != d:
+                    continue
+                ring(h, w, d, step - 1).wait_recv()
+                if step < 3 or (step == 3 and w == d):
+                    go(ring(h, w, d, step))
+            if step > 1:
+                spread(h, w, step - 2)
+
+    for w in range(2):
+        for d in range(2):
+            near_in(w, 2 - 4 * d)
+            go(relay(w, d, False))
+            if w == d:
+                go(relay(w, d, True))
+    for h in range(1, HPD):
+        first_step(h)
+    for w in range(2):
+        own_audio(EARLY, w).wait()
+        for dz in (0, 1, -1):
+            near_in(w, dz)
+        spread(EARLY, w, 0)
+    for h in range(1, HPD):
+        next_step(h, 1)
+    send_video(1)
+    for w in range(2):
+        for d in range(2):
+            relay(w, d, False).wait_recv()
+        relay(w, w, True).wait_recv()
+        spread(EARLY, w, 1)
+        spread(EARLY, w, 2)
 
     pltpu.make_async_copy(mine, lists_v.at[x], own_i.at[0]).wait()
     for peer in peers():
@@ -327,7 +373,7 @@
         return remote(final[h].at[w, to], outs[w].at[:, head_cols(mine_at, h)], (f_send, f_recv), (h, w, r), (c, to, z))
 
     def own_final(h, w):
-        return pltpu.make_async_copy(final[h].at[w, x], outs[w].at[:, head_cols(x, h)], own_f.at[h, w])
+        return pltpu.make_async_copy(final[h].at[w, x], outs[w].at[:, head_cols(x, h)], own_f.at[h, w, 0])
 
     def finish(h):
         for w in range(2):
@@ -353,17 +399,88 @@
         place(h)
         hand_out(h)
 
+    def home_copy(w, rel, r, to, mine_at):
+        where = (c, to, (z + rel + NZ) % NZ)
+        return remote(leaving.at[w, at(rel), to], home.at[w, mine_at, at(-rel)], (h_send, h_recv), (w, at(rel), r), where)
+
+    def send_home(w, rel, value):
+        leaving[w, at(rel)] = value.astype(BF16)
+        for r, to, _ in near_peers(rel):
+            go(home_copy(w, rel, r, to, x))
+        if rel == 0:
+            home[w, x, 0] = leaving[w, 0, x]
+
+    def last_ring(w, d, dist):
+        sign, slot = 1 - 2 * d, (w, d, dist - 1)
+        where = (c, x, (z + sign * (dist - 2) + NZ) % NZ)
+        return remote(moving[LATE].at[slot], landed[LATE].at[slot], (s_send, s_recv), (LATE, *slot), where)
+
+    def last_far():
+        for w in range(2):
+            edges_in(LATE, w, 0)
+            for dist in (4, 3):
+                for d in range(2):
+                    if dist == 3 or w == d:
+                        moving[LATE][w, d, dist - 1] = total(LATE, w, -dist if d else dist).astype(BF16)
+                        go(last_ring(w, d, dist))
+
+    def last_near():
+        for w in range(2):
+            edges_in(LATE, w, 1)
+            for rel in (1, -1, 0):
+                send_home(w, rel, total(LATE, w, rel))
+
+    def last_two():
+        for w in range(2):
+            for d in range(2):
+                rel = -2 if d else 2
+                last_ring(w, d, 3).wait_recv()
+                value = total(LATE, w, rel) + landed[LATE][w, d, 2].astype(jnp.float32)
+                if w == d:
+                    last_ring(w, d, 4).wait_recv()
+                    value = value + landed[LATE][w, d, 3].astype(jnp.float32)
+                send_home(w, rel, value)
+
+    def own_last(w, line):
+        return pltpu.make_async_copy(final[LATE].at[w, line], outs[w].at[:, head_cols(line, LATE)], own_f.at[LATE, w, line])
+
+    def last_finish():
+        for w in range(2):
+            for rel in (0, 1, -1, 2, -2):
+                for r, to, came in near_peers(rel):
+                    home_copy(w, rel, r, to, came).wait_recv()
+            value = home[w, :, 0].astype(jnp.float32)
+            for i in range(1, 2 * REACH + 1):
+                value = value + home[w, :, i].astype(jnp.float32)
+            final[LATE][w] = value.astype(BF16)
+            for line in range(NX):
+                own_last(w, line).start()
+
+    def steps(step):
+        for h in range(1, HPD):
+            next_step(h, step)
+
+    steps(2)
     compute(0)
+    send_video(2)
+    steps(3)
+    sums(0, 4)
+    steps(4)
+    sums(0, 3)
     compute(1)
-    sums(0, 4)
+    sums(0, 2)
     compute(2)
     sums(1, 4)
-    sums(2, 4)
-    for dist in (3, 2, 1):
-        for h in range(HPD):
-            sums(h, dist)
-    for h in range(HPD):
-        finish(h)
+    sums(0, 1)
+    sums(1, 3)
+    last_far()
+    finish(0)
+    sums(1, 2)
+    last_near()
+    last_two()
+    sums(1, 1)
+    finish(1)
+    last_finish()
 
     for h in range(HPD):
         own_query(h).wait()
@@ -372,9 +489,13 @@
             query_copy(h, r, to, came).wait_recv()
         for w in range(2):
             spread_wait(h, w, True)
-            own_final(h, w).wait()
-            for r, to, came in peers():
-                final_copy(h, w, r, to, came).wait_recv()
+            if h == LATE:
+                for line in range(NX):
+                    own_last(w, line).wait()
+            else:
+                own_final(h, w).wait()
+                for r, to, came in peers():
+                    final_copy(h, w, r, to, came).wait_recv()
 
             for part_of in range(len(EDGES)):
 
@@ -422,16 +543,19 @@
             pltpu.VMEM((NX, 8, 128), jnp.int32),
             pltpu.SMEM((NX, 8, 128), jnp.int32),
             pltpu.SMEM((2, TILES), jnp.int32),
+            pltpu.VMEM((2, 2 * REACH + 1, NX, ROWS, HDIM), BF16),
+            pltpu.VMEM((2, NX, 2 * REACH + 1, ROWS, HDIM), BF16),
             *sems(HPD, 2, NX - 1), *sems(NX - 1), *sems(HPD, 2, NX - 1), *sems(HPD, 2, 2, 4), *sems(HPD, 2, 2, len(SPREADS)),
             *sems(HPD, NX - 1), *sems(HPD, 2, 2, len(EDGES)), *sems(HPD, 2, 2, 4), *sems(HPD, 2, NX - 1),
+            *sems(2, 2 * REACH + 1, NX), *sems(2, 2 * REACH + 1, NX),
             pltpu.SemaphoreType.DMA((HPD, 2)),
             pltpu.SemaphoreType.DMA((HPD, 2)),
             pltpu.SemaphoreType.DMA((HPD,)),
-            pltpu.SemaphoreType.DMA((HPD, 2)),
+            pltpu.SemaphoreType.DMA((HPD, 2, NX)),
             pltpu.SemaphoreType.DMA((2,)),
         ],
         compiler_params=pltpu.CompilerParams(
-            collective_id=0, has_side_effects=True, vmem_limit_bytes=48 * 2**20
+            collective_id=0, has_side_effects=True, vmem_limit_bytes=62 * 2**20
         ),
         name="cross_attention_backward",
     )(q, g, k, v, lists)

time: 71.6 us -> 72.8 us (1.017)
  Pallas kernels: 63.5 us -> 68.3 us
  local copies, waits for them, and re-layouts: 6.88 us -> 3.67 us
    pallas_call x1, Pallas kernels: 63.5 us -> 68.3 us  [per_device(): pl.pallas_call(kernel, out_shape=tuple((jax.ShapeDtypeStruct(a.shape, BF1...]
    unnamed x13 -> x7, local copies, waits for them, and re-layouts: 6.88 us -> 3.67 us
where the time goes in v4:
time: 72.8 us; the launch traced here: 72.6 us
  Pallas kernels  68.3 us (94%)
  local copies, waits for them, and re-layouts  3.67 us (5%)
    pallas_call x1, Pallas kernels, per_device(): pl.pallas_call(kernel, out_shape=tuple((jax.ShapeDtypeStruct(a.shape, BF1...  68.3 us
    unnamed x7, local copies, waits for them, and re-layouts  3.67 us

profile of v4, /device:TPU:8, one launch (start us, length us, event | category | flops | bytes accessed | tf_op | source)
XLA Modules:
  0.0 72.6 jit_solution(15611815744765571716)
XLA Ops:
  0.6 68.3 %cross_attention_backward.1 = (bf16[256,1536]{1,0:T(8,128)(2,1)}, bf16[32,1536]{1,0:T(8,128)(2,1)}, bf16[32,1536]{1,0:T(8,128)(2,1)}) custom-call(bf16[256,1536]{1,0:T(8,128)(2,1)} %q.1, bf16[256,1536]{1,0:T(8,128)(2,1)} %g.1, bf16[32,1536]{1,0:T(8,128)(2,1)} %k.1, bf16[32,1536]{1,0:T(8,128)(2,1)} %v.1, s32[2,8]{1,0:T(2,128)} %lists.1), custom_call_target="tpu_custom_call" | custom-call | tf_op jit(solution)/shard_map/cross_attention_backward/pallas_call | solution.py:527
  69.0 0.0 copy-start.1
  69.0 2.1 %copy.11 = bf16[256,1536]{1,0:T(8,128)(2,1)} copy(bf16[256,1536]{1,0:T(8,128)(2,1)} %get-tuple-element.6) | data formatting | bytes 1572864
  71.1 0.0 copy-done.1
  71.1 0.0 copy-start
  71.1 0.6 copy.12
  71.7 0.3 copy-done
  72.0 0.6 copy.13
Async XLA Ops:
  69.0 2.1 %copy-start.1 = (bf16[32,1536]{1,0:T(8,128)(2,1)S(1)}, bf16[32,1536]{1,0:T(8,128)(2,1)}, u32[]{:S(2)}) copy-start(bf16[32,1536]{1,0:T(8,128)(2,1)} %get-tuple-element.7) | copy-start | bytes 294916
  71.1 0.9 %copy-start = (bf16[32,1536]{1,0:T(8,128)(2,1)S(1)}, bf16[32,1536]{1,0:T(8,128)(2,1)}, u32[]{:S(2)}) copy-start(bf16[32,1536]{1,0:T(8,128)(2,1)} %get-tuple-element.8) | copy-start | bytes 294916

commit v5 on v3

v5 whole, which is shorter than its diff:
```python
import jax
import jax.numpy as jnp
from jax import lax
from jax.experimental import pallas as pl
from jax.experimental.pallas import tpu as pltpu
from jax.sharding import PartitionSpec as P

MESH = pl.DeviceIdType.MESH
HEADS = 12
HDIM = 128
NX, NZ, NC = 4, 8, 8
HPD = HEADS // NX
ROWS = 32
VROWS = 256
VBLK = 128
LMAX = 8
KEYS = LMAX * ROWS
WIN = 2 * NX * NZ
TILES = 2 * NX
REACH = 2
EARLY, LATE = 0, HPD - 1
SPREADS = ((0, 5), (5, 2), (7, 1))
EDGES = ((5, 3), (0, 5))
MASKED = -1e30
LOG2E = 1.4426950408889634
BF16 = jnp.bfloat16


def dev(c, x, z):
    return {"grp": c, "seq": x * NZ + z}


def enter(c, x, z):
    barrier = pltpu.get_barrier_semaphore()

    def greet(*where):
        pl.semaphore_signal(barrier, inc=1, device_id=dev(*where), device_id_type=MESH)

    for dz in range(-REACH, REACH + 1):
        for r in range(NX):
            if dz or r:
                greet(c, (x + r) % NX, (z + dz + NZ) % NZ)

    @pl.when(c > 0)
    def _():
        greet(c - 1, x, z)

    @pl.when(c < NC - 1)
    def _():
        greet(c + 1, x, z)

    inner = jnp.logical_and(c > 0, c < NC - 1)
    pl.semaphore_wait(barrier, NX * (2 * REACH + 1) - 1 + 1 + inner.astype(jnp.int32))


def remote(src, dst, send, recv, where):
    return pltpu.make_async_remote_copy(
        src_ref=src, dst_ref=dst, send_sem=send, recv_sem=recv, device_id=dev(*where), device_id_type=MESH
    )


def local(src, dst, sem):
    return pltpu.make_async_copy(src, dst, sem)


def at(rel):
    return NZ - 1 if abs(rel) == 4 else 2 * rel if rel >= 0 else -2 * rel - 1


def head_cols(x, h):
    return pl.ds(pl.multiple_of((x * HPD + h) * HDIM, HDIM), HDIM)


def nt(a, b):
    return lax.dot_general(a, b, (((1,), (1,)), ((), ())), preferred_element_type=jnp.float32)


def tn(a, b):
    return lax.dot_general(a, b, (((0,), (0,)), ((), ())), preferred_element_type=jnp.float32)


def nn(a, b):
    return lax.dot_general(a, b, (((1,), (0,)), ((), ())), preferred_element_type=jnp.float32)


def kernel(
    q, g, k, v, lists, out_q, out_k, out_v,
    kv0, kv1, kv2, qg0, qg1, qg2, dq0, dq1, dq2, part0, part1, part2, edge0, edge1, edge2,
    moving0, moving1, moving2, landed0, landed1, landed2, final0, final1, final2,
    pads, mine, lists_v, lists_s, runs, leaving, home,
    sent, up_sent, down_sent, near_sem, audio_sem, video_sem, ring_sem, spread_sem, edge_sem, sum_sem, out_sem, home_sem, list_sem,
):
    c, s = lax.axis_index("grp"), lax.axis_index("seq")
    x, z = s // NZ, s % NZ
    enter(c, x, z)
    audio, video, outs = (k, v), (q, g), (out_k, out_v)
    kv, qg, dq = (kv0, kv1, kv2), (qg0, qg1, qg2), (dq0, dq1, dq2)
    part, edge = (part0, part1, part2), (edge0, edge1, edge2)
    moving, landed, final = (moving0, moving1, moving2), (landed0, landed1, landed2), (final0, final1, final2)
    above, below = jnp.minimum(c + 1, NC - 1), jnp.maximum(c - 1, 0)
    has_above, has_below = c < NC - 1, c > 0
    NEAR, AUDIO, VIDEO, LIST, RING, SUM, QUERY, FINAL, HOME = (sent.at[i] for i in range(9))

    def awaited(ref, sem):
        local(ref, ref, sem).wait()

    def peers():
        return [(x + r) % NX for r in range(1, NX)]

    def along(sign, hops):
        return (c, x, (z + sign * hops + NZ) % NZ)

    def send_near():
        for w in range(2):
            for dz in (2, -2, 1, -1, 0):
                for r in range(NX):
                    to = (x + r) % NX
                    source, target = audio[w].at[:, head_cols(to, EARLY)], kv[EARLY].at[w, 2 + x, at(-dz)]
                    if dz or r:
                        remote(source, target, NEAR, near_sem.at[at(dz)], (c, to, (z + dz + NZ) % NZ)).start()
                    else:
                        local(source, target, near_sem.at[0]).start()

    def near_in(dz):
        awaited(kv[EARLY].at[:, pl.ds(2, NX), at(-dz)], near_sem.at[at(dz)])

    def send_audio(h):
        for w in range(2):
            for to in peers():
                source, target = audio[w].at[:, head_cols(to, h)], kv[h].at[w, 2 + x, 0]
                remote(source, target, AUDIO, audio_sem.at[h], (c, to, z)).start()
            local(audio[w].at[:, head_cols(x, h)], kv[h].at[w, 2 + x, 0], audio_sem.at[h]).start()

    def send_video(h):
        for w in range(2):
            for to in peers():
                source, target = video[w].at[:, head_cols(to, h)], qg[h].at[w, x]
                remote(source, target, VIDEO, video_sem.at[h], (c, to, z)).start()
            local(video[w].at[:, head_cols(x, h)], qg[h].at[w, x], video_sem.at[h]).start()

    def onward(h, d, far, hops, slot, whole):
        sign = 1 - 2 * d
        what = pl.ds(0, 2) if whole else pl.ds(d, 1)
        source = kv[h].at[what, pl.ds(2, NX), at(-sign * far)]
        target = kv[h].at[what, pl.ds(2, NX), at(-sign * (far + hops))]
        return remote(source, target, RING, ring_sem.at[h, d, slot], along(sign, hops))

    def spread(h, low, count):
        span = pl.ds(low, count)

        @pl.when(has_above)
        def _():
            source, target = kv[h].at[:, pl.ds(4, 2), span], kv[h].at[:, pl.ds(0, 2), span]
            remote(source, target, up_sent.at[0], spread_sem.at[h, 0], (above, x, z)).start()

        @pl.when(has_below)
        def _():
            source, target = kv[h].at[:, pl.ds(2, 2), span], kv[h].at[:, pl.ds(6, 2), span]
            remote(source, target, down_sent.at[0], spread_sem.at[h, 1], (below, x, z)).start()

    def ready(h):
        awaited(qg[h], video_sem.at[h])

        @pl.when(has_above)
        def _():
            awaited(kv[h].at[:, pl.ds(6, 2)], spread_sem.at[h, 1])

        @pl.when(has_below)
        def _():
            awaited(kv[h].at[:, pl.ds(0, 2)], spread_sem.at[h, 0])

    def first_step(h):
        awaited(kv[h].at[:, pl.ds(2, NX), 0], audio_sem.at[h])
        for d in range(2):
            onward(h, d, 0, 1, 0, True).start()

    def next_step(h, step):
        for d in range(2):
            onward(h, d, step - 1, 1, step - 1, step < 4).wait_recv()
            if step < 4:
                onward(h, d, step, 1, step, step < 3).start()
        if step > 1:
            spread(h, *SPREADS[step - 2])

    send_near()
    for h in range(1, HPD):
        send_audio(h)
    mine[...] = jnp.zeros_like(mine)
    mine[0:2, 0:LMAX] = lists[...]
    for to in peers():
        remote(mine, lists_v.at[x], LIST, list_sem.at[0], (c, to, z)).start()
    local(mine, lists_v.at[x], list_sem.at[0]).start()
    send_video(EARLY)
    pads[:, :, 0:LMAX] = jnp.zeros((TILES, 2, LMAX, ROWS, HDIM), jnp.float32)
    pads[:, :, 2 * LMAX : 3 * LMAX] = jnp.zeros((TILES, 2, LMAX, ROWS, HDIM), jnp.float32)
    for h in range(HPD):

        @pl.when(c == 0)
        def _():
            edge[h][:, 0] = jnp.zeros((2,) + edge[h].shape[2:], BF16)

        @pl.when(c == NC - 1)
        def _():
            edge[h][:, 1] = jnp.zeros((2,) + edge[h].shape[2:], BF16)

    for d in range(2):
        near_in(2 - 4 * d)
        onward(EARLY, d, 2, 1, 0, True).start()
        onward(EARLY, d, 2, 2, 1, False).start()
    for h in range(1, HPD):
        first_step(h)
    for dz in (0, 1, -1):
        near_in(dz)
    spread(EARLY, 0, 5)
    for h in range(1, HPD):
        next_step(h, 1)
    send_video(1)
    for d in range(2):
        onward(EARLY, d, 2, 1, 0, True).wait_recv()
        onward(EARLY, d, 2, 2, 1, False).wait_recv()
    spread(EARLY, 5, 3)

    awaited(lists_v, list_sem.at[0])
    fetched = local(lists_v, lists_s, list_sem.at[1])
    fetched.start()
    fetched.wait()
    for t in range(TILES):
        count = jnp.int32(0)
        for j in range(LMAX):
            count += (lists_s[t // 2, t % 2, j] >= 0).astype(jnp.int32)
        runs[0, t] = jnp.clip(lists_s[t // 2, t % 2, 0] - (c * NX * NZ - NX * NZ // 2), 0, WIN - 1)
        runs[1, t] = count

    scale = HDIM**-0.5

    def tiles(h):
        loaded, ready_terms = [], []
        for t in range(TILES):
            first, count = runs[0, t], runs[1, t]
            blocks = [jnp.minimum(first + jnp.where(j < count, j, 0), WIN - 1) for j in range(LMAX)]
            places = [(e >> 3, ((e & 7) - z + NZ) & 7) for e in blocks]
            places = [(line, jnp.where(rel < 4, 2 * rel, 15 - 2 * rel)) for line, rel in places]
            kt = jnp.concatenate([kv[h][0, line, where] for line, where in places], axis=0)
            vt = jnp.concatenate([kv[h][1, line, where] for line, where in places], axis=0)
            rows = pl.ds(t % 2 * VBLK, VBLK)
            qt, gt = qg[h][0, t // 2, rows], qg[h][1, t // 2, rows]
            loaded.append((count, kt, qt, gt, nt(kt, qt), nt(vt, gt)))
        for count, kt, qt, gt, products, grad_weights in loaded:
            dead = [jnp.full((ROWS, VBLK), jnp.where(j < count, 0.0, MASKED), jnp.float32) for j in range(LMAX)]
            scores = products * (scale * LOG2E) + jnp.concatenate(dead, axis=0)
            raw = jnp.exp2(scores - jnp.max(scores, axis=0, keepdims=True))
            inverse = 1.0 / jnp.sum(raw, axis=0, keepdims=True)
            inner = jnp.sum(raw * grad_weights, axis=0, keepdims=True) * inverse
            weights_low = (raw * inverse).astype(BF16)
            grad_scores = (raw * ((grad_weights - inner) * (inverse * scale))).astype(BF16)
            ready_terms.append((kt, qt, gt, weights_low, grad_scores))
        for t, (kt, qt, gt, weights_low, grad_scores) in enumerate(ready_terms):
            pads[t, 1, LMAX : 2 * LMAX] = nn(weights_low, gt).reshape(LMAX, ROWS, HDIM)
            pads[t, 0, LMAX : 2 * LMAX] = nn(grad_scores, qt).reshape(LMAX, ROWS, HDIM)
            dq[h][t // 2, pl.ds(t % 2 * VBLK, VBLK)] = tn(grad_scores, kt).astype(BF16)

    def place(h):
        for w in range(2):
            for line in range(2 * NX):
                near = range(max(0, line - NX) * 2, min(NX, line + 1) * 2)
                total = None
                for t in near:
                    term = pads[t, w, pl.ds(jnp.clip(line * NZ - runs[0, t] + LMAX, 0, 2 * LMAX), LMAX)]
                    total = term if total is None else total + term
                total = total.astype(BF16)
                for zz in range(NZ):
                    rel = (zz - z + NZ) & 7
                    part[h][w, line, jnp.where(rel < 4, 2 * rel, 15 - 2 * rel)] = total[zz]

    def edge_copy(h, d, part_of):
        low, count = EDGES[part_of]
        line, to, sem = ((6, above, up_sent), (0, below, down_sent))[d]
        source, target = part[h].at[:, pl.ds(line, 2), pl.ds(low, count)], edge[h].at[:, d, :, pl.ds(low, count)]
        return remote(source, target, sem.at[1], edge_sem.at[h, d, part_of], (to, x, z))

    def hand_out(h):
        for part_of in range(len(EDGES)):

            @pl.when(has_above)
            def _():
                edge_copy(h, 0, part_of).start()

            @pl.when(has_below)
            def _():
                edge_copy(h, 1, part_of).start()

        for to in peers():
            remote(dq[h].at[to], out_q.at[:, head_cols(x, h)], QUERY, out_sem.at[2], (c, to, z)).start()
        local(dq[h].at[x], out_q.at[:, head_cols(x, h)], out_sem.at[2]).start()

    def edges_in(h, part_of):
        @pl.when(has_above)
        def _():
            edge_copy(h, 1, part_of).wait_recv()

        @pl.when(has_below)
        def _():
            edge_copy(h, 0, part_of).wait_recv()

    def total(h, w, rel):
        p = at(rel)
        low = part[h][w, 2:4, p].astype(jnp.float32) + edge[h][w, 0, :, p].astype(jnp.float32)
        high = part[h][w, 4:6, p].astype(jnp.float32) + edge[h][w, 1, :, p].astype(jnp.float32)
        return jnp.concatenate([low, high], axis=0)

    def sum_copy(h, d, dist, hops):
        what = pl.ds(0, 2) if dist < 4 else pl.ds(d, 1)
        source, target = moving[h].at[d, dist - 1, what], landed[h].at[d, dist - 1, what]
        return remote(source, target, SUM, sum_sem.at[h, d, dist - 1], along(1 - 2 * d, hops))

    def sums(h, dist):
        if dist in (4, 2):
            edges_in(h, 0 if dist == 4 else 1)
        for d in range(2):
            if dist < 4:
                sum_copy(h, d, dist + 1, 1).wait_recv()
            for w in range(2):
                if dist == 4 and w != d:
                    continue
                value = total(h, w, -dist if d else dist)
                if dist < 3 or (dist == 3 and w == d):
                    value = value + landed[h][d, dist, w].astype(jnp.float32)
                moving[h][d, dist - 1, w] = value.astype(BF16)
            sum_copy(h, d, dist, 1).start()

    def finish(h):
        for d in range(2):
            sum_copy(h, d, 1, 1).wait_recv()
        for w in range(2):
            value = total(h, w, 0)
            for d in range(2):
                value = value + landed[h][d, 0, w].astype(jnp.float32)
            final[h][w] = value.astype(BF16)
            target = outs[w].at[:, head_cols(x, h)]
            for to in peers():
                remote(final[h].at[w, to], target, FINAL, out_sem.at[w], (c, to, z)).start()
            local(final[h].at[w, x], target, out_sem.at[w]).start()

    def send_home(w, rel, value):
        leaving[w, at(rel)] = value.astype(BF16)
        for r in range(NX):
            to = (x + r) % NX
            source, target = leaving.at[w, at(rel), to], home.at[w, x, at(-rel)]
            if rel or r:
                remote(source, target, HOME, home_sem.at[0], (c, to, (z + rel + NZ) % NZ)).start()
            else:
                local(source, target, home_sem.at[0]).start()

    def last_far():
        edges_in(LATE, 0)
        for dist in (4, 3):
            for d in range(2):
                for w in range(2):
                    if dist == 3 or w == d:
                        moving[LATE][d, dist - 1, w] = total(LATE, w, -dist if d else dist).astype(BF16)
                sum_copy(LATE, d, dist, dist - 2).start()

    def last_near():
        edges_in(LATE, 1)
        for w in range(2):
            for rel in (1, -1, 0):
                send_home(w, rel, total(LATE, w, rel))

    def last_two():
        for d in range(2):
            for dist in (3, 4):
                sum_copy(LATE, d, dist, dist - 2).wait_recv()
            for w in range(2):
                rel = -2 if d else 2
                value = total(LATE, w, rel) + landed[LATE][d, 2, w].astype(jnp.float32)
                if w == d:
                    value = value + landed[LATE][d, 3, w].astype(jnp.float32)
                send_home(w, rel, value)

    def last_finish():
        awaited(home, home_sem.at[0])
        for w in range(2):
            value = home[w, :, 0].astype(jnp.float32)
            for i in range(1, 2 * REACH + 1):
                value = value + home[w, :, i].astype(jnp.float32)
            final[LATE][w] = value.astype(BF16)
            for line in range(NX):
                local(final[LATE].at[w, line], outs[w].at[:, head_cols(line, LATE)], out_sem.at[w]).start()

    def compute(h):
        ready(h)
        tiles(h)
        place(h)
        hand_out(h)

    def steps(step):
        for h in range(1, HPD):
            next_step(h, step)

    steps(2)
    compute(0)
    send_video(2)
    steps(3)
    sums(0, 4)
    steps(4)
    sums(0, 3)
    compute(1)
    sums(0, 2)
    compute(2)
    sums(1, 4)
    sums(0, 1)
    sums(1, 3)
    last_far()
    finish(0)
    sums(1, 2)
    last_near()
    last_two()
    sums(1, 1)
    finish(1)
    last_finish()

    awaited(out_q, out_sem.at[2])
    for w in range(2):
        awaited(outs[w], out_sem.at[w])
    for i in range(2):

        @pl.when(has_above)
        def _():
            awaited(pads.at[pl.ds(0, 2), 0], up_sent.at[i])

        @pl.when(has_below)
        def _():
            awaited(pads.at[pl.ds(0, 2), 0], down_sent.at[i])

    for sem, a, b in ((NEAR, 1, 19), (AUDIO, 1, 6), (VIDEO, 3, 24), (RING, 4, 17), (SUM, 4, 17), (QUERY, 3, 12), (FINAL, 1, 6), (HOME, 1, 19)):
        awaited(pads.at[pl.ds(0, a), 0, pl.ds(0, b)], sem)
    awaited(lists_v.at[pl.ds(0, NX - 1)], LIST)


HBM = pl.BlockSpec(memory_space=pltpu.HBM)
VMEM = pl.BlockSpec(memory_space=pltpu.VMEM)


def sems(*shape):
    return pltpu.SemaphoreType.DMA(shape)


def each(*shape):
    return [pltpu.VMEM(shape, BF16)] * HPD


def per_device(q, k, v, g, lists):
    return pl.pallas_call(
        kernel,
        out_shape=tuple(jax.ShapeDtypeStruct(a.shape, BF16) for a in (q, k, v)),
        in_specs=[HBM] * 4 + [VMEM],
        out_specs=(HBM,) * 3,
        scratch_shapes=[
            *each(2, 2 * NX, NZ, ROWS, HDIM),
            *each(2, NX, VROWS, HDIM),
            *each(NX, VROWS, HDIM),
            *each(2, 2 * NX, NZ, ROWS, HDIM),
            *each(2, 2, 2, NZ, ROWS, HDIM),
            *each(2, 4, 2, NX, ROWS, HDIM),
            *each(2, 4, 2, NX, ROWS, HDIM),
            *each(2, NX, ROWS, HDIM),
            pltpu.VMEM((TILES, 2, 3 * LMAX, ROWS, HDIM), jnp.float32),
            pltpu.VMEM((8, 128), jnp.int32),
            pltpu.VMEM((NX, 8, 128), jnp.int32),
            pltpu.SMEM((NX, 8, 128), jnp.int32),
            pltpu.SMEM((2, TILES), jnp.int32),
            pltpu.VMEM((2, 2 * REACH + 1, NX, ROWS, HDIM), BF16),
            pltpu.VMEM((2, NX, 2 * REACH + 1, ROWS, HDIM), BF16),
            sems(9), sems(2), sems(2), sems(2 * REACH + 1), sems(HPD), sems(HPD), sems(HPD, 2, 4), sems(HPD, 2),
            sems(HPD, 2, len(EDGES)), sems(HPD, 2, 4), sems(3), sems(1), sems(2),
        ],
        compiler_params=pltpu.CompilerParams(
            collective_id=0, has_side_effects=True, vmem_limit_bytes=62 * 2**20
        ),
        name="cross_attention_backward",
    )(q, g, k, v, lists)


def solution(mesh):
    placed = P(("grp", "seq"), None)
    return jax.shard_map(
        per_device,
        mesh=mesh,
        in_specs=(placed,) * 5,
        out_specs=(placed,) * 3,
        check_vma=False,
    )
```

time: 71.6 us -> 68.8 us (0.961)
  local copies, waits for them, and re-layouts: 6.88 us -> 3.67 us
  Pallas kernels: 63.5 us -> 64.3 us
    unnamed x13 -> x7, local copies, waits for them, and re-layouts: 6.88 us -> 3.67 us
    pallas_call x1, Pallas kernels: 63.5 us -> 64.3 us  [per_device(): pl.pallas_call(kernel, out_shape=tuple((jax.ShapeDtypeStruct(a.shape, BF1...]
where the time goes in v5:
time: 68.8 us; the launch traced here: 68.6 us
  Pallas kernels  64.3 us (93%)
  local copies, waits for them, and re-layouts  3.67 us (5%)
    pallas_call x1, Pallas kernels, per_device(): pl.pallas_call(kernel, out_shape=tuple((jax.ShapeDtypeStruct(a.shape, BF1...  64.3 us
    unnamed x7, local copies, waits for them, and re-layouts  3.67 us

profile of v5, /device:TPU:8, one launch (start us, length us, event | category | flops | bytes accessed | tf_op | source)
XLA Modules:
  0.0 68.6 jit_solution(12085787613603471541)
XLA Ops:
  0.6 64.3 %cross_attention_backward.1 = (bf16[256,1536]{1,0:T(8,128)(2,1)}, bf16[32,1536]{1,0:T(8,128)(2,1)}, bf16[32,1536]{1,0:T(8,128)(2,1)}) custom-call(bf16[256,1536]{1,0:T(8,128)(2,1)} %q.1, bf16[256,1536]{1,0:T(8,128)(2,1)} %g.1, bf16[32,1536]{1,0:T(8,128)(2,1)} %k.1, bf16[32,1536]{1,0:T(8,128)(2,1)} %v.1, s32[2,8]{1,0:T(2,128)} %lists.1), custom_call_target="tpu_custom_call" | custom-call | tf_op jit(solution)/shard_map/cross_attention_backward/pallas_call | solution.py:453
  65.0 0.0 copy-start.1
  65.0 2.1 %copy.11 = bf16[256,1536]{1,0:T(8,128)(2,1)} copy(bf16[256,1536]{1,0:T(8,128)(2,1)} %get-tuple-element.6) | data formatting | bytes 1572864
  67.1 0.0 copy-done.1
  67.1 0.0 copy-start
  67.1 0.6 copy.12
  67.7 0.3 copy-done
  68.0 0.6 copy.13
Async XLA Ops:
  65.0 2.1 %copy-start.1 = (bf16[32,1536]{1,0:T(8,128)(2,1)S(1)}, bf16[32,1536]{1,0:T(8,128)(2,1)}, u32[]{:S(2)}) copy-start(bf16[32,1536]{1,0:T(8,128)(2,1)} %get-tuple-element.7) | copy-start | bytes 294916
  67.1 0.9 %copy-start = (bf16[32,1536]{1,0:T(8,128)(2,1)S(1)}, bf16[32,1536]{1,0:T(8,128)(2,1)}, u32[]{:S(2)}) copy-start(bf16[32,1536]{1,0:T(8,128)(2,1)} %get-tuple-element.8) | copy-start | bytes 294916

commit v6 on v5

--- a/solution.py
+++ b/solution.py
@@ -17,15 +17,28 @@
 KEYS = LMAX * ROWS
 WIN = 2 * NX * NZ
 TILES = 2 * NX
-REACH = 2
-EARLY, LATE = 0, HPD - 1
+LATE = HPD - 1
+HOMING = True
+PIECES = ((0, 2),)
 SPREADS = ((0, 5), (5, 2), (7, 1))
-EDGES = ((5, 3), (0, 5))
+EDGES = ((7, 1), (5, 2), (0, 5))
 MASKED = -1e30
 LOG2E = 1.4426950408889634
 BF16 = jnp.bfloat16
 
 
+SCHEDULE = (
+    ("audio", 0), ("audio", 1), ("audio", 2), ("lists",), ("video", 0),
+    ("there", 0, 0), ("there", 1, 0), ("there", 2, 0), ("clear",), ("there", 0, 1), ("there", 1, 1), ("there", 2, 1),
+    ("video", 1), ("there", 0, 2), ("there", 1, 2), ("there", 2, 2), ("video", 2), ("there", 0, 3), ("there", 1, 3),
+    ("there", 2, 3), ("read",), ("there", 0, 4), ("there", 1, 4), ("there", 2, 4),
+    ("compute", 0), ("compute", 1), ("compute", 2), ("edges", 0), ("edges", 1), ("edges", 2),
+    ("back", 0, 4), ("back", 1, 4), ("back", 2, 4),
+    ("back", 0, 3), ("back", 1, 3), ("back", 2, 3), ("back", 0, 2), ("back", 1, 2), ("back", 2, 2),
+    ("back", 0, 1), ("back", 1, 1), ("back", 2, 1), ("back", 0, 0), ("back", 1, 0), ("back", 2, 0),
+)
+
+
 def dev(c, x, z):
     return {"grp": c, "seq": x * NZ + z}
 
@@ -36,10 +49,9 @@
     def greet(*where):
         pl.semaphore_signal(barrier, inc=1, device_id=dev(*where), device_id_type=MESH)
 
-    for dz in range(-REACH, REACH + 1):
-        for r in range(NX):
-            if dz or r:
-                greet(c, (x + r) % NX, (z + dz + NZ) % NZ)
+    peers = [(r, dz) for dz in (-1, 0, 1) for r in range(NX) if (r or dz) and (HOMING or not r or not dz)]
+    for r, dz in peers:
+        greet(c, (x + r) % NX, (z + dz + NZ) % NZ)
 
     @pl.when(c > 0)
     def _():
@@ -50,7 +62,7 @@
         greet(c + 1, x, z)
 
     inner = jnp.logical_and(c > 0, c < NC - 1)
-    pl.semaphore_wait(barrier, NX * (2 * REACH + 1) - 1 + 1 + inner.astype(jnp.int32))
+    pl.semaphore_wait(barrier, len(peers) + 1 + inner.astype(jnp.int32))
 
 
 def remote(src, dst, send, recv, where):
@@ -88,7 +100,7 @@
     kv0, kv1, kv2, qg0, qg1, qg2, dq0, dq1, dq2, part0, part1, part2, edge0, edge1, edge2,
     moving0, moving1, moving2, landed0, landed1, landed2, final0, final1, final2,
     pads, mine, lists_v, lists_s, runs, leaving, home,
-    sent, up_sent, down_sent, near_sem, audio_sem, video_sem, ring_sem, spread_sem, edge_sem, sum_sem, out_sem, home_sem, list_sem,
+    sent, up_sent, down_sent, audio_sem, video_sem, ring_sem, spread_sem, edge_sem, sum_sem, out_sem, home_sem, list_sem,
 ):
     c, s = lax.axis_index("grp"), lax.axis_index("seq")
     x, z = s // NZ, s % NZ
@@ -99,7 +111,7 @@
     moving, landed, final = (moving0, moving1, moving2), (landed0, landed1, landed2), (final0, final1, final2)
     above, below = jnp.minimum(c + 1, NC - 1), jnp.maximum(c - 1, 0)
     has_above, has_below = c < NC - 1, c > 0
-    NEAR, AUDIO, VIDEO, LIST, RING, SUM, QUERY, FINAL, HOME = (sent.at[i] for i in range(9))
+    AUDIO, VIDEO, LIST, RING, SUM, QUERY, FINAL, HOME = (sent.at[i] for i in range(8))
 
     def awaited(ref, sem):
         local(ref, ref, sem).wait()
@@ -109,20 +121,6 @@
 
     def along(sign, hops):
         return (c, x, (z + sign * hops + NZ) % NZ)
-
-    def send_near():
-        for w in range(2):
-            for dz in (2, -2, 1, -1, 0):
-                for r in range(NX):
-                    to = (x + r) % NX
-                    source, target = audio[w].at[:, head_cols(to, EARLY)], kv[EARLY].at[w, 2 + x, at(-dz)]
-                    if dz or r:
-                        remote(source, target, NEAR, near_sem.at[at(dz)], (c, to, (z + dz + NZ) % NZ)).start()
-                    else:
-                        local(source, target, near_sem.at[0]).start()
-
-    def near_in(dz):
-        awaited(kv[EARLY].at[:, pl.ds(2, NX), at(-dz)], near_sem.at[at(dz)])
 
     def send_audio(h):
         for w in range(2):
@@ -138,12 +136,12 @@
                 remote(source, target, VIDEO, video_sem.at[h], (c, to, z)).start()
             local(video[w].at[:, head_cols(x, h)], qg[h].at[w, x], video_sem.at[h]).start()
 
-    def onward(h, d, far, hops, slot, whole):
+    def onward(h, d, step, piece):
         sign = 1 - 2 * d
-        what = pl.ds(0, 2) if whole else pl.ds(d, 1)
-        source = kv[h].at[what, pl.ds(2, NX), at(-sign * far)]
-        target = kv[h].at[what, pl.ds(2, NX), at(-sign * (far + hops))]
-        return remote(source, target, RING, ring_sem.at[h, d, slot], along(sign, hops))
+        what = pl.ds(*piece) if step < 3 else pl.ds(d, 1)
+        source = kv[h].at[what, pl.ds(2, NX), at(-sign * step)]
+        target = kv[h].at[what, pl.ds(2, NX), at(-sign * (step + 1))]
+        return remote(source, target, RING, ring_sem.at[h, d, step, piece[0]], along(sign, 1))
 
     def spread(h, low, count):
         span = pl.ds(low, count)
@@ -169,67 +167,50 @@
         def _():
             awaited(kv[h].at[:, pl.ds(0, 2)], spread_sem.at[h, 0])
 
-    def first_step(h):
-        awaited(kv[h].at[:, pl.ds(2, NX), 0], audio_sem.at[h])
-        for d in range(2):
-            onward(h, d, 0, 1, 0, True).start()
-
-    def next_step(h, step):
-        for d in range(2):
-            onward(h, d, step - 1, 1, step - 1, step < 4).wait_recv()
-            if step < 4:
-                onward(h, d, step, 1, step, step < 3).start()
+    def there(h, step):
+        if step == 0:
+            awaited(kv[h].at[:, pl.ds(2, NX), 0], audio_sem.at[h])
+        for piece in PIECES:
+            for d in range(2):
+                ends = d in range(piece[0], sum(piece))
+                if step and (step < 4 or ends):
+                    onward(h, d, step - 1, piece).wait_recv()
+                if step < 3 or (step == 3 and ends):
+                    onward(h, d, step, piece).start()
         if step > 1:
             spread(h, *SPREADS[step - 2])
 
-    send_near()
-    for h in range(1, HPD):
-        send_audio(h)
-    mine[...] = jnp.zeros_like(mine)
-    mine[0:2, 0:LMAX] = lists[...]
-    for to in peers():
-        remote(mine, lists_v.at[x], LIST, list_sem.at[0], (c, to, z)).start()
-    local(mine, lists_v.at[x], list_sem.at[0]).start()
-    send_video(EARLY)
-    pads[:, :, 0:LMAX] = jnp.zeros((TILES, 2, LMAX, ROWS, HDIM), jnp.float32)
-    pads[:, :, 2 * LMAX : 3 * LMAX] = jnp.zeros((TILES, 2, LMAX, ROWS, HDIM), jnp.float32)
-    for h in range(HPD):
-
-        @pl.when(c == 0)
-        def _():
-            edge[h][:, 0] = jnp.zeros((2,) + edge[h].shape[2:], BF16)
-
-        @pl.when(c == NC - 1)
-        def _():
-            edge[h][:, 1] = jnp.zeros((2,) + edge[h].shape[2:], BF16)
-
-    for d in range(2):
-        near_in(2 - 4 * d)
-        onward(EARLY, d, 2, 1, 0, True).start()
-        onward(EARLY, d, 2, 2, 1, False).start()
-    for h in range(1, HPD):
-        first_step(h)
-    for dz in (0, 1, -1):
-        near_in(dz)
-    spread(EARLY, 0, 5)
-    for h in range(1, HPD):
-        next_step(h, 1)
-    send_video(1)
-    for d in range(2):
-        onward(EARLY, d, 2, 1, 0, True).wait_recv()
-        onward(EARLY, d, 2, 2, 1, False).wait_recv()
-    spread(EARLY, 5, 3)
-
-    awaited(lists_v, list_sem.at[0])
-    fetched = local(lists_v, lists_s, list_sem.at[1])
-    fetched.start()
-    fetched.wait()
-    for t in range(TILES):
-        count = jnp.int32(0)
-        for j in range(LMAX):
-            count += (lists_s[t // 2, t % 2, j] >= 0).astype(jnp.int32)
-        runs[0, t] = jnp.clip(lists_s[t // 2, t % 2, 0] - (c * NX * NZ - NX * NZ // 2), 0, WIN - 1)
-        runs[1, t] = count
+    def send_lists():
+        mine[...] = jnp.zeros_like(mine)
+        mine[0:2, 0:LMAX] = lists[...]
+        for to in peers():
+            remote(mine, lists_v.at[x], LIST, list_sem.at[0], (c, to, z)).start()
+        local(mine, lists_v.at[x], list_sem.at[0]).start()
+
+    def clear():
+        pads[:, :, 0:LMAX] = jnp.zeros((TILES, 2, LMAX, ROWS, HDIM), jnp.float32)
+        pads[:, :, 2 * LMAX : 3 * LMAX] = jnp.zeros((TILES, 2, LMAX, ROWS, HDIM), jnp.float32)
+        for h in range(HPD):
+
+            @pl.when(c == 0)
+            def _():
+                edge[h][:, 0] = jnp.zeros((2,) + edge[h].shape[2:], BF16)
+
+            @pl.when(c == NC - 1)
+            def _():
+                edge[h][:, 1] = jnp.zeros((2,) + edge[h].shape[2:], BF16)
+
+    def read_lists():
+        awaited(lists_v, list_sem.at[0])
+        fetched = local(lists_v, lists_s, list_sem.at[1])
+        fetched.start()
+        fetched.wait()
+        for t in range(TILES):
+            count = jnp.int32(0)
+            for j in range(LMAX):
+                count += (lists_s[t // 2, t % 2, j] >= 0).astype(jnp.int32)
+            runs[0, t] = jnp.clip(lists_s[t // 2, t % 2, 0] - (c * NX * NZ - NX * NZ // 2), 0, WIN - 1)
+            runs[1, t] = count
 
     scale = HDIM**-0.5
 
@@ -278,17 +259,16 @@
         source, target = part[h].at[:, pl.ds(line, 2), pl.ds(low, count)], edge[h].at[:, d, :, pl.ds(low, count)]
         return remote(source, target, sem.at[1], edge_sem.at[h, d, part_of], (to, x, z))
 
-    def hand_out(h):
-        for part_of in range(len(EDGES)):
-
-            @pl.when(has_above)
-            def _():
-                edge_copy(h, 0, part_of).start()
-
-            @pl.when(has_below)
-            def _():
-                edge_copy(h, 1, part_of).start()
-
+    def send_edges(h, part_of):
+        @pl.when(has_above)
+        def _():
+            edge_copy(h, 0, part_of).start()
+
+        @pl.when(has_below)
+        def _():
+            edge_copy(h, 1, part_of).start()
+
+    def send_queries(h):
         for to in peers():
             remote(dq[h].at[to], out_q.at[:, head_cols(x, h)], QUERY, out_sem.at[2], (c, to, z)).start()
         local(dq[h].at[x], out_q.at[:, head_cols(x, h)], out_sem.at[2]).start()
@@ -308,29 +288,38 @@
         high = part[h][w, 4:6, p].astype(jnp.float32) + edge[h][w, 1, :, p].astype(jnp.float32)
         return jnp.concatenate([low, high], axis=0)
 
-    def sum_copy(h, d, dist, hops):
-        what = pl.ds(0, 2) if dist < 4 else pl.ds(d, 1)
+    def sum_copy(h, d, dist, piece):
+        what = pl.ds(*piece) if dist < 4 else pl.ds(d, 1)
         source, target = moving[h].at[d, dist - 1, what], landed[h].at[d, dist - 1, what]
-        return remote(source, target, SUM, sum_sem.at[h, d, dist - 1], along(1 - 2 * d, hops))
+        return remote(source, target, SUM, sum_sem.at[h, d, dist - 1, piece[0]], along(1 - 2 * d, 1))
 
     def sums(h, dist):
-        if dist in (4, 2):
-            edges_in(h, 0 if dist == 4 else 1)
-        for d in range(2):
-            if dist < 4:
-                sum_copy(h, d, dist + 1, 1).wait_recv()
-            for w in range(2):
-                if dist == 4 and w != d:
+        if dist > 1:
+            edges_in(h, 4 - dist)
+        for piece in PIECES:
+            for d in range(2):
+                ends = d in range(piece[0], sum(piece))
+                if dist == 4 and not ends:
                     continue
-                value = total(h, w, -dist if d else dist)
-                if dist < 3 or (dist == 3 and w == d):
-                    value = value + landed[h][d, dist, w].astype(jnp.float32)
-                moving[h][d, dist - 1, w] = value.astype(BF16)
-            sum_copy(h, d, dist, 1).start()
+                if dist < 3 or (dist == 3 and ends):
+                    sum_copy(h, d, dist + 1, piece).wait_recv()
+                for w in range(piece[0], sum(piece)):
+                    if dist == 4 and w != d:
+                        continue
+                    value = total(h, w, -dist if d else dist)
+                    if dist < 3 or (dist == 3 and w == d):
+                        value = value + landed[h][d, dist, w].astype(jnp.float32)
+                    if HOMING and h == LATE and dist == 1:
+                        send_home(w, 1 - 2 * d, value)
+                    else:
+                        moving[h][d, dist - 1, w] = value.astype(BF16)
+                if not (HOMING and h == LATE and dist == 1):
+                    sum_copy(h, d, dist, piece).start()
 
     def finish(h):
-        for d in range(2):
-            sum_copy(h, d, 1, 1).wait_recv()
+        for piece in PIECES:
+            for d in range(2):
+                sum_copy(h, d, 1, piece).wait_recv()
         for w in range(2):
             value = total(h, w, 0)
             for d in range(2):
@@ -351,37 +340,11 @@
             else:
                 local(source, target, home_sem.at[0]).start()
 
-    def last_far():
-        edges_in(LATE, 0)
-        for dist in (4, 3):
-            for d in range(2):
-                for w in range(2):
-                    if dist == 3 or w == d:
-                        moving[LATE][d, dist - 1, w] = total(LATE, w, -dist if d else dist).astype(BF16)
-                sum_copy(LATE, d, dist, dist - 2).start()
-
-    def last_near():
-        edges_in(LATE, 1)
-        for w in range(2):
-            for rel in (1, -1, 0):
-                send_home(w, rel, total(LATE, w, rel))
-
-    def last_two():
-        for d in range(2):
-            for dist in (3, 4):
-                sum_copy(LATE, d, dist, dist - 2).wait_recv()
-            for w in range(2):
-                rel = -2 if d else 2
-                value = total(LATE, w, rel) + landed[LATE][d, 2, w].astype(jnp.float32)
-                if w == d:
-                    value = value + landed[LATE][d, 3, w].astype(jnp.float32)
-                send_home(w, rel, value)
-
     def last_finish():
         awaited(home, home_sem.at[0])
         for w in range(2):
             value = home[w, :, 0].astype(jnp.float32)
-            for i in range(1, 2 * REACH + 1):
+            for i in range(1, 3):
                 value = value + home[w, :, i].astype(jnp.float32)
             final[LATE][w] = value.astype(BF16)
             for line in range(NX):
@@ -391,33 +354,29 @@
         ready(h)
         tiles(h)
         place(h)
-        hand_out(h)
-
-    def steps(step):
-        for h in range(1, HPD):
-            next_step(h, step)
-
-    steps(2)
-    compute(0)
-    send_video(2)
-    steps(3)
-    sums(0, 4)
-    steps(4)
-    sums(0, 3)
-    compute(1)
-    sums(0, 2)
-    compute(2)
-    sums(1, 4)
-    sums(0, 1)
-    sums(1, 3)
-    last_far()
-    finish(0)
-    sums(1, 2)
-    last_near()
-    last_two()
-    sums(1, 1)
-    finish(1)
-    last_finish()
+        send_edges(h, 0)
+        send_edges(h, 1)
+        send_queries(h)
+
+    def back(h, dist):
+        if HOMING and h == LATE and dist == 1:
+            for w in range(2):
+                send_home(w, 0, total(h, w, 0))
+        if dist:
+            sums(h, dist)
+        elif HOMING and h == LATE:
+            last_finish()
+        else:
+            finish(h)
+
+    def edges(h):
+        send_edges(h, 2)
+
+    for action, *arguments in SCHEDULE:
+        {
+            "audio": send_audio, "video": send_video, "lists": send_lists, "clear": clear, "read": read_lists,
+            "there": there, "compute": compute, "edges": edges, "back": back,
+        }[action](*arguments)
 
     awaited(out_q, out_sem.at[2])
     for w in range(2):
@@ -432,8 +391,13 @@
         def _():
             awaited(pads.at[pl.ds(0, 2), 0], down_sent.at[i])
 
-    for sem, a, b in ((NEAR, 1, 19), (AUDIO, 1, 6), (VIDEO, 3, 24), (RING, 4, 17), (SUM, 4, 17), (QUERY, 3, 12), (FINAL, 1, 6), (HOME, 1, 19)):
-        awaited(pads.at[pl.ds(0, a), 0, pl.ds(0, b)], sem)
+    homing = 1 if HOMING else 0
+    for sem, a, b in (
+        (AUDIO, 1, 9), (VIDEO, 3, 24), (RING, 4, 21), (SUM, 4, 21 - 2 * homing), (QUERY, 3, 12), (FINAL, 1, 9 - 3 * homing),
+        (HOME, 1, 11 * homing),
+    ):
+        if b:
+            awaited(pads.at[pl.ds(0, a), 0, pl.ds(0, b)], sem)
     awaited(lists_v.at[pl.ds(0, NX - 1)], LIST)
 
 
@@ -469,10 +433,10 @@
             pltpu.VMEM((NX, 8, 128), jnp.int32),
             pltpu.SMEM((NX, 8, 128), jnp.int32),
             pltpu.SMEM((2, TILES), jnp.int32),
-            pltpu.VMEM((2, 2 * REACH + 1, NX, ROWS, HDIM), BF16),
-            pltpu.VMEM((2, NX, 2 * REACH + 1, ROWS, HDIM), BF16),
-            sems(9), sems(2), sems(2), sems(2 * REACH + 1), sems(HPD), sems(HPD), sems(HPD, 2, 4), sems(HPD, 2),
-            sems(HPD, 2, len(EDGES)), sems(HPD, 2, 4), sems(3), sems(1), sems(2),
+            pltpu.VMEM((2, 3, NX, ROWS, HDIM), BF16),
+            pltpu.VMEM((2, NX, 3, ROWS, HDIM), BF16),
+            sems(8), sems(2), sems(2), sems(HPD), sems(HPD), sems(HPD, 2, 4, len(PIECES)), sems(HPD, 2),
+            sems(HPD, 2, len(EDGES)), sems(HPD, 2, 4, len(PIECES)), sems(3), sems(1), sems(2),
         ],
         compiler_params=pltpu.CompilerParams(
             collective_id=0, has_side_effects=True, vmem_limit_bytes=62 * 2**20

time: 68.8 us -> 64.6 us (0.939)
  Pallas kernels: 64.3 us -> 59.6 us
    pallas_call x1, Pallas kernels: 64.3 us -> 59.6 us  [per_device(): pl.pallas_call(kernel, out_shape=tuple((jax.ShapeDtypeStruct(a.shape, BF1...]
where the time goes in v6:
time: 64.6 us; the launch traced here: 63.9 us
  Pallas kernels  59.6 us (92%)
  local copies, waits for them, and re-layouts  3.67 us (6%)
  between operations  0.65 us (1%)
    pallas_call x1, Pallas kernels, per_device(): pl.pallas_call(kernel, out_shape=tuple((jax.ShapeDtypeStruct(a.shape, BF1...  59.6 us
    unnamed x7, local copies, waits for them, and re-layouts  3.67 us

profile of v6, /device:TPU:8, one launch (start us, length us, event | category | flops | bytes accessed | tf_op | source)
XLA Modules:
  0.0 63.9 jit_solution(8865229416595829137)
XLA Ops:
  0.6 59.6 %cross_attention_backward.1 = (bf16[256,1536]{1,0:T(8,128)(2,1)}, bf16[32,1536]{1,0:T(8,128)(2,1)}, bf16[32,1536]{1,0:T(8,128)(2,1)}) custom-call(bf16[256,1536]{1,0:T(8,128)(2,1)} %q.1, bf16[256,1536]{1,0:T(8,128)(2,1)} %g.1, bf16[32,1536]{1,0:T(8,128)(2,1)} %k.1, bf16[32,1536]{1,0:T(8,128)(2,1)} %v.1, s32[2,8]{1,0:T(2,128)} %lists.1), custom_call_target="tpu_custom_call" | custom-call | tf_op jit(solution)/shard_map/cross_attention_backward/pallas_call | solution.py:417
  60.2 0.0 copy-start.1
  60.2 2.1 %copy.11 = bf16[256,1536]{1,0:T(8,128)(2,1)} copy(bf16[256,1536]{1,0:T(8,128)(2,1)} %get-tuple-element.6) | data formatting | bytes 1572864
  62.3 0.0 copy-done.1
  62.3 0.0 copy-start
  62.3 0.6 %copy.12 = bf16[32,1536]{1,0:T(8,128)(2,1)} copy(bf16[32,1536]{1,0:T(8,128)(2,1)S(1)} %copy-done.1) | data formatting | bytes 196608
  63.0 0.3 copy-done
  63.3 0.6 %copy.13 = bf16[32,1536]{1,0:T(8,128)(2,1)} copy(bf16[32,1536]{1,0:T(8,128)(2,1)S(1)} %copy-done) | data formatting | bytes 196608
Async XLA Ops:
  60.2 2.1 %copy-start.1 = (bf16[32,1536]{1,0:T(8,128)(2,1)S(1)}, bf16[32,1536]{1,0:T(8,128)(2,1)}, u32[]{:S(2)}) copy-start(bf16[32,1536]{1,0:T(8,128)(2,1)} %get-tuple-element.7) | copy-start | bytes 294916
  62.3 0.9 %copy-start = (bf16[32,1536]{1,0:T(8,128)(2,1)S(1)}, bf16[32,1536]{1,0:T(8,128)(2,1)}, u32[]{:S(2)}) copy-start(bf16[32,1536]{1,0:T(8,128)(2,1)} %get-tuple-element.8) | copy-start | bytes 294916

commit v7 on v6

--- a/solution.py
+++ b/solution.py
@@ -17,9 +17,6 @@
 KEYS = LMAX * ROWS
 WIN = 2 * NX * NZ
 TILES = 2 * NX
-LATE = HPD - 1
-HOMING = True
-PIECES = ((0, 2),)
 SPREADS = ((0, 5), (5, 2), (7, 1))
 EDGES = ((7, 1), (5, 2), (0, 5))
 MASKED = -1e30
@@ -29,13 +26,13 @@
 
 SCHEDULE = (
     ("audio", 0), ("audio", 1), ("audio", 2), ("lists",), ("video", 0),
-    ("there", 0, 0), ("there", 1, 0), ("there", 2, 0), ("clear",), ("there", 0, 1), ("there", 1, 1), ("there", 2, 1),
+    ("clear",), ("there", 0, 1), ("there", 1, 1), ("there", 2, 1),
     ("video", 1), ("there", 0, 2), ("there", 1, 2), ("there", 2, 2), ("video", 2), ("there", 0, 3), ("there", 1, 3),
     ("there", 2, 3), ("read",), ("there", 0, 4), ("there", 1, 4), ("there", 2, 4),
     ("compute", 0), ("compute", 1), ("compute", 2), ("edges", 0), ("edges", 1), ("edges", 2),
     ("back", 0, 4), ("back", 1, 4), ("back", 2, 4),
     ("back", 0, 3), ("back", 1, 3), ("back", 2, 3), ("back", 0, 2), ("back", 1, 2), ("back", 2, 2),
-    ("back", 0, 1), ("back", 1, 1), ("back", 2, 1), ("back", 0, 0), ("back", 1, 0), ("back", 2, 0),
+    ("own", 0), ("own", 1), ("own", 2), ("back", 0, 1), ("back", 1, 1), ("back", 2, 1), ("finish", 0), ("finish", 1), ("finish", 2),
 )
 
 
@@ -49,7 +46,7 @@
     def greet(*where):
         pl.semaphore_signal(barrier, inc=1, device_id=dev(*where), device_id_type=MESH)
 
-    peers = [(r, dz) for dz in (-1, 0, 1) for r in range(NX) if (r or dz) and (HOMING or not r or not dz)]
+    peers = [(r, dz) for dz in (-1, 0, 1) for r in range(NX) if r or dz]
     for r, dz in peers:
         greet(c, (x + r) % NX, (z + dz + NZ) % NZ)
 
@@ -99,7 +96,7 @@
     q, g, k, v, lists, out_q, out_k, out_v,
     kv0, kv1, kv2, qg0, qg1, qg2, dq0, dq1, dq2, part0, part1, part2, edge0, edge1, edge2,
     moving0, moving1, moving2, landed0, landed1, landed2, final0, final1, final2,
-    pads, mine, lists_v, lists_s, runs, leaving, home,
+    pads, mine, lists_v, lists_s, runs, leaving, home0, home1, home2,
     sent, up_sent, down_sent, audio_sem, video_sem, ring_sem, spread_sem, edge_sem, sum_sem, out_sem, home_sem, list_sem,
 ):
     c, s = lax.axis_index("grp"), lax.axis_index("seq")
@@ -109,9 +106,10 @@
     kv, qg, dq = (kv0, kv1, kv2), (qg0, qg1, qg2), (dq0, dq1, dq2)
     part, edge = (part0, part1, part2), (edge0, edge1, edge2)
     moving, landed, final = (moving0, moving1, moving2), (landed0, landed1, landed2), (final0, final1, final2)
+    home = (home0, home1, home2)
     above, below = jnp.minimum(c + 1, NC - 1), jnp.maximum(c - 1, 0)
     has_above, has_below = c < NC - 1, c > 0
-    AUDIO, VIDEO, LIST, RING, SUM, QUERY, FINAL, HOME = (sent.at[i] for i in range(8))
+    AUDIO, VIDEO, LIST, RING, SUM, QUERY, HOME = (sent.at[i] for i in range(7))
 
     def awaited(ref, sem):
         local(ref, ref, sem).wait()
@@ -124,10 +122,17 @@
 
     def send_audio(h):
         for w in range(2):
-            for to in peers():
-                source, target = audio[w].at[:, head_cols(to, h)], kv[h].at[w, 2 + x, 0]
-                remote(source, target, AUDIO, audio_sem.at[h], (c, to, z)).start()
-            local(audio[w].at[:, head_cols(x, h)], kv[h].at[w, 2 + x, 0], audio_sem.at[h]).start()
+            for dz in (1, -1, 0):
+                for r in range(NX):
+                    to = (x + r) % NX
+                    source, target = audio[w].at[:, head_cols(to, h)], kv[h].at[w, 2 + x, at(-dz)]
+                    if dz or r:
+                        remote(source, target, AUDIO, audio_sem.at[h, at(dz)], (c, to, (z + dz + NZ) % NZ)).start()
+                    else:
+                        local(source, target, audio_sem.at[h, 0]).start()
+
+    def audio_in(h, dz):
+        awaited(kv[h].at[:, pl.ds(2, NX), at(-dz)], audio_sem.at[h, at(dz)])
 
     def send_video(h):
         for w in range(2):
@@ -136,12 +141,12 @@
                 remote(source, target, VIDEO, video_sem.at[h], (c, to, z)).start()
             local(video[w].at[:, head_cols(x, h)], qg[h].at[w, x], video_sem.at[h]).start()
 
-    def onward(h, d, step, piece):
+    def onward(h, d, step):
         sign = 1 - 2 * d
-        what = pl.ds(*piece) if step < 3 else pl.ds(d, 1)
+        what = pl.ds(0, 2) if step < 3 else pl.ds(d, 1)
         source = kv[h].at[what, pl.ds(2, NX), at(-sign * step)]
         target = kv[h].at[what, pl.ds(2, NX), at(-sign * (step + 1))]
-        return remote(source, target, RING, ring_sem.at[h, d, step, piece[0]], along(sign, 1))
+        return remote(source, target, RING, ring_sem.at[h, d, step - 1], along(sign, 1))
 
     def spread(h, low, count):
         span = pl.ds(low, count)
@@ -168,15 +173,15 @@
             awaited(kv[h].at[:, pl.ds(0, 2)], spread_sem.at[h, 0])
 
     def there(h, step):
-        if step == 0:
-            awaited(kv[h].at[:, pl.ds(2, NX), 0], audio_sem.at[h])
-        for piece in PIECES:
-            for d in range(2):
-                ends = d in range(piece[0], sum(piece))
-                if step and (step < 4 or ends):
-                    onward(h, d, step - 1, piece).wait_recv()
-                if step < 3 or (step == 3 and ends):
-                    onward(h, d, step, piece).start()
+        for d in range(2):
+            if step == 1:
+                audio_in(h, 1 - 2 * d)
+            else:
+                onward(h, d, step - 1).wait_recv()
+            if step < 4:
+                onward(h, d, step).start()
+        if step == 2:
+            audio_in(h, 0)
         if step > 1:
             spread(h, *SPREADS[step - 2])
 
@@ -288,67 +293,53 @@
         high = part[h][w, 4:6, p].astype(jnp.float32) + edge[h][w, 1, :, p].astype(jnp.float32)
         return jnp.concatenate([low, high], axis=0)
 
-    def sum_copy(h, d, dist, piece):
-        what = pl.ds(*piece) if dist < 4 else pl.ds(d, 1)
-        source, target = moving[h].at[d, dist - 1, what], landed[h].at[d, dist - 1, what]
-        return remote(source, target, SUM, sum_sem.at[h, d, dist - 1, piece[0]], along(1 - 2 * d, 1))
-
-    def sums(h, dist):
+    def sum_copy(h, d, dist):
+        what = pl.ds(0, 2) if dist < 4 else pl.ds(d, 1)
+        source, target = moving[h].at[d, dist - 2, what], landed[h].at[d, dist - 2, what]
+        return remote(source, target, SUM, sum_sem.at[h, d, dist - 2], along(1 - 2 * d, 1))
+
+    def send_home(h, w, rel, value):
+        leaving[h, w, at(rel)] = value.astype(BF16)
+        for r in range(NX):
+            to = (x + r) % NX
+            source, target = leaving.at[h, w, at(rel), to], home[h].at[w, x, at(-rel)]
+            if rel or r:
+                remote(source, target, HOME, home_sem.at[h], (c, to, (z + rel + NZ) % NZ)).start()
+            else:
+                local(source, target, home_sem.at[h]).start()
+
+    def back(h, dist):
         if dist > 1:
             edges_in(h, 4 - dist)
-        for piece in PIECES:
-            for d in range(2):
-                ends = d in range(piece[0], sum(piece))
-                if dist == 4 and not ends:
+        for d in range(2):
+            if dist < 4:
+                sum_copy(h, d, dist + 1).wait_recv()
+            for w in range(2):
+                if dist == 4 and w != d:
                     continue
-                if dist < 3 or (dist == 3 and ends):
-                    sum_copy(h, d, dist + 1, piece).wait_recv()
-                for w in range(piece[0], sum(piece)):
-                    if dist == 4 and w != d:
-                        continue
-                    value = total(h, w, -dist if d else dist)
-                    if dist < 3 or (dist == 3 and w == d):
-                        value = value + landed[h][d, dist, w].astype(jnp.float32)
-                    if HOMING and h == LATE and dist == 1:
-                        send_home(w, 1 - 2 * d, value)
-                    else:
-                        moving[h][d, dist - 1, w] = value.astype(BF16)
-                if not (HOMING and h == LATE and dist == 1):
-                    sum_copy(h, d, dist, piece).start()
+                value = total(h, w, -dist if d else dist)
+                if dist < 3 or (dist == 3 and w == d):
+                    value = value + landed[h][d, dist - 1, w].astype(jnp.float32)
+                if dist == 1:
+                    send_home(h, w, 1 - 2 * d, value)
+                else:
+                    moving[h][d, dist - 2, w] = value.astype(BF16)
+            if dist > 1:
+                sum_copy(h, d, dist).start()
+
+    def own(h):
+        for w in range(2):
+            send_home(h, w, 0, total(h, w, 0))
 
     def finish(h):
-        for piece in PIECES:
-            for d in range(2):
-                sum_copy(h, d, 1, piece).wait_recv()
+        awaited(home[h], home_sem.at[h])
         for w in range(2):
-            value = total(h, w, 0)
-            for d in range(2):
-                value = value + landed[h][d, 0, w].astype(jnp.float32)
+            value = home[h][w, :, 0].astype(jnp.float32)
+            for i in range(1, 3):
+                value = value + home[h][w, :, i].astype(jnp.float32)
             final[h][w] = value.astype(BF16)
-            target = outs[w].at[:, head_cols(x, h)]
-            for to in peers():
-                remote(final[h].at[w, to], target, FINAL, out_sem.at[w], (c, to, z)).start()
-            local(final[h].at[w, x], target, out_sem.at[w]).start()
-
-    def send_home(w, rel, value):
-        leaving[w, at(rel)] = value.astype(BF16)
-        for r in range(NX):
-            to = (x + r) % NX
-            source, target = leaving.at[w, at(rel), to], home.at[w, x, at(-rel)]
-            if rel or r:
-                remote(source, target, HOME, home_sem.at[0], (c, to, (z + rel + NZ) % NZ)).start()
-            else:
-                local(source, target, home_sem.at[0]).start()
-
-    def last_finish():
-        awaited(home, home_sem.at[0])
-        for w in range(2):
-            value = home[w, :, 0].astype(jnp.float32)
-            for i in range(1, 3):
-                value = value + home[w, :, i].astype(jnp.float32)
-            final[LATE][w] = value.astype(BF16)
             for line in range(NX):
-                local(final[LATE].at[w, line], outs[w].at[:, head_cols(line, LATE)], out_sem.at[w]).start()
+                local(final[h].at[w, line], outs[w].at[:, head_cols(line, h)], out_sem.at[w]).start()
 
     def compute(h):
         ready(h)
@@ -358,24 +349,13 @@
         send_edges(h, 1)
         send_queries(h)
 
-    def back(h, dist):
-        if HOMING and h == LATE and dist == 1:
-            for w in range(2):
-                send_home(w, 0, total(h, w, 0))
-        if dist:
-            sums(h, dist)
-        elif HOMING and h == LATE:
-            last_finish()
-        else:
-            finish(h)
-
     def edges(h):
         send_edges(h, 2)
 
     for action, *arguments in SCHEDULE:
         {
             "audio": send_audio, "video": send_video, "lists": send_lists, "clear": clear, "read": read_lists,
-            "there": there, "compute": compute, "edges": edges, "back": back,
+            "there": there, "compute": compute, "edges": edges, "back": back, "own": own, "finish": finish,
         }[action](*arguments)
 
     awaited(out_q, out_sem.at[2])
@@ -391,14 +371,27 @@
         def _():
             awaited(pads.at[pl.ds(0, 2), 0], down_sent.at[i])
 
-    homing = 1 if HOMING else 0
-    for sem, a, b in (
-        (AUDIO, 1, 9), (VIDEO, 3, 24), (RING, 4, 21), (SUM, 4, 21 - 2 * homing), (QUERY, 3, 12), (FINAL, 1, 9 - 3 * homing),
-        (HOME, 1, 11 * homing),
-    ):
-        if b:
-            awaited(pads.at[pl.ds(0, a), 0, pl.ds(0, b)], sem)
+    for sem, a, b in ((AUDIO, 3, 11), (VIDEO, 3, 24), (RING, 3, 20), (SUM, 3, 20), (QUERY, 3, 12), (HOME, 3, 11)):
+        awaited(pads.at[pl.ds(0, a), 0, pl.ds(0, b)], sem)
     awaited(lists_v.at[pl.ds(0, NX - 1)], LIST)
+
+
+def copy_kernel(q, k, v, out_q, out_k, out_v, held_q, held_k, held_v, sem):
+    half = VROWS // 2
+    low, high = pl.ds(0, half), pl.ds(half, half)
+    ways = (
+        (q.at[low], held_q.at[low], out_q.at[low]), (q.at[high], held_q.at[high], out_q.at[high]),
+        (k, held_k, out_k), (v, held_v, out_v),
+    )
+    first = [local(a, b, sem.at[0, i]) for i, (a, b, _) in enumerate(ways)]
+    second = [local(b, o, sem.at[1, i]) for i, (_, b, o) in enumerate(ways)]
+    for copy in first:
+        copy.start()
+    for one, two in zip(first, second):
+        one.wait()
+        two.start()
+    for copy in second:
+        copy.wait()
 
 
 HBM = pl.BlockSpec(memory_space=pltpu.HBM)
@@ -414,7 +407,7 @@
 
 
 def per_device(q, k, v, g, lists):
-    return pl.pallas_call(
+    grads = pl.pallas_call(
         kernel,
         out_shape=tuple(jax.ShapeDtypeStruct(a.shape, BF16) for a in (q, k, v)),
         in_specs=[HBM] * 4 + [VMEM],
@@ -425,24 +418,32 @@
             *each(NX, VROWS, HDIM),
             *each(2, 2 * NX, NZ, ROWS, HDIM),
             *each(2, 2, 2, NZ, ROWS, HDIM),
-            *each(2, 4, 2, NX, ROWS, HDIM),
-            *each(2, 4, 2, NX, ROWS, HDIM),
+            *each(2, 3, 2, NX, ROWS, HDIM),
+            *each(2, 3, 2, NX, ROWS, HDIM),
             *each(2, NX, ROWS, HDIM),
             pltpu.VMEM((TILES, 2, 3 * LMAX, ROWS, HDIM), jnp.float32),
             pltpu.VMEM((8, 128), jnp.int32),
             pltpu.VMEM((NX, 8, 128), jnp.int32),
             pltpu.SMEM((NX, 8, 128), jnp.int32),
             pltpu.SMEM((2, TILES), jnp.int32),
-            pltpu.VMEM((2, 3, NX, ROWS, HDIM), BF16),
-            pltpu.VMEM((2, NX, 3, ROWS, HDIM), BF16),
-            sems(8), sems(2), sems(2), sems(HPD), sems(HPD), sems(HPD, 2, 4, len(PIECES)), sems(HPD, 2),
-            sems(HPD, 2, len(EDGES)), sems(HPD, 2, 4, len(PIECES)), sems(3), sems(1), sems(2),
+            pltpu.VMEM((HPD, 2, 3, NX, ROWS, HDIM), BF16),
+            *each(2, NX, 3, ROWS, HDIM),
+            sems(7), sems(2), sems(2), sems(HPD, 3), sems(HPD), sems(HPD, 2, 3), sems(HPD, 2),
+            sems(HPD, 2, len(EDGES)), sems(HPD, 2, 3), sems(3), sems(HPD), sems(2),
         ],
         compiler_params=pltpu.CompilerParams(
             collective_id=0, has_side_effects=True, vmem_limit_bytes=62 * 2**20
         ),
         name="cross_attention_backward",
     )(q, g, k, v, lists)
+    return pl.pallas_call(
+        copy_kernel,
+        out_shape=tuple(jax.ShapeDtypeStruct(a.shape, BF16) for a in (q, k, v)),
+        in_specs=[HBM] * 3,
+        out_specs=(HBM,) * 3,
+        scratch_shapes=[*(pltpu.VMEM(a.shape, BF16) for a in (q, k, v)), sems(2, 4)],
+        name="final_copies",
+    )(*grads)
 
 
 def solution(mesh):

time: 64.6 us -> 62.7 us (0.971)
  the two profiles are of different devices: /device:TPU:8 before, /device:TPU:1 now
where the time goes in v7:
time: 62.7 us; the launch traced here: 62.6 us
  Pallas kernels  62 us (99%)
  between operations  0.64 us (1%)
    pallas_call x1, Pallas kernels, per_device(): pl.pallas_call(kernel, out_shape=tuple((jax.ShapeDtypeStruct(a.shape, BF1...  60 us
    pallas_call x1, Pallas kernels, per_device(): pl.pallas_call(copy_kernel, out_shape=tuple((jax.ShapeDtypeStruct(a.shape...  2 us

profile of v7, /device:TPU:1, one launch (start us, length us, event | category | flops | bytes accessed | tf_op | source)
XLA Modules:
  0.0 62.6 jit_solution(2439946547873751485)
XLA Ops:
  0.6 60.0 %cross_attention_backward.1 = (bf16[256,1536]{1,0:T(8,128)(2,1)}, bf16[32,1536]{1,0:T(8,128)(2,1)}, bf16[32,1536]{1,0:T(8,128)(2,1)}) custom-call(bf16[256,1536]{1,0:T(8,128)(2,1)} %q.1, bf16[256,1536]{1,0:T(8,128)(2,1)} %g.1, bf16[32,1536]{1,0:T(8,128)(2,1)} %k.1, bf16[32,1536]{1,0:T(8,128)(2,1)} %v.1, s32[2,8]{1,0:T(2,128)} %lists.1), custom_call_target="tpu_custom_call" | custom-call | tf_op jit(solution)/shard_map/cross_attention_backward/pallas_call | solution.py:410
  60.6 2.0 %final_copies.1 = (bf16[256,1536]{1,0:T(8,128)(2,1)}, bf16[32,1536]{1,0:T(8,128)(2,1)}, bf16[32,1536]{1,0:T(8,128)(2,1)}) custom-call(bf16[256,1536]{1,0:T(8,128)(2,1)} %get-tuple-element.6.q, bf16[32,1536]{1,0:T(8,128)(2,1)} %get-tuple-element.7.k, bf16[32,1536]{1,0:T(8,128)(2,1)} %get-tuple-element.8.v), custom_call_target="tpu_custom_call" | custom-call | tf_op jit(solution)/shard_map/final_copies/pallas_call | solution.py:439

commit v8 on v7

--- a/solution.py
+++ b/solution.py
@@ -17,6 +17,7 @@
 KEYS = LMAX * ROWS
 WIN = 2 * NX * NZ
 TILES = 2 * NX
+NEAR = 1
 SPREADS = ((0, 5), (5, 2), (7, 1))
 EDGES = ((7, 1), (5, 2), (0, 5))
 MASKED = -1e30
@@ -25,7 +26,7 @@
 
 
 SCHEDULE = (
-    ("audio", 0), ("audio", 1), ("audio", 2), ("lists",), ("video", 0),
+    ("audio", 0), ("audio", 1), ("audio", 2), ("there", 1, 0), ("there", 2, 0), ("lists",), ("video", 0),
     ("clear",), ("there", 0, 1), ("there", 1, 1), ("there", 2, 1),
     ("video", 1), ("there", 0, 2), ("there", 1, 2), ("there", 2, 2), ("video", 2), ("there", 0, 3), ("there", 1, 3),
     ("there", 2, 3), ("read",), ("there", 0, 4), ("there", 1, 4), ("there", 2, 4),
@@ -122,7 +123,7 @@
 
     def send_audio(h):
         for w in range(2):
-            for dz in (1, -1, 0):
+            for dz in (1, -1, 0) if h < NEAR else (0,):
                 for r in range(NX):
                     to = (x + r) % NX
                     source, target = audio[w].at[:, head_cols(to, h)], kv[h].at[w, 2 + x, at(-dz)]
@@ -146,7 +147,7 @@
         what = pl.ds(0, 2) if step < 3 else pl.ds(d, 1)
         source = kv[h].at[what, pl.ds(2, NX), at(-sign * step)]
         target = kv[h].at[what, pl.ds(2, NX), at(-sign * (step + 1))]
-        return remote(source, target, RING, ring_sem.at[h, d, step - 1], along(sign, 1))
+        return remote(source, target, RING, ring_sem.at[h, d, step], along(sign, 1))
 
     def spread(h, low, count):
         span = pl.ds(low, count)
@@ -173,14 +174,19 @@
             awaited(kv[h].at[:, pl.ds(0, 2)], spread_sem.at[h, 0])
 
     def there(h, step):
+        if step == 0:
+            audio_in(h, 0)
         for d in range(2):
-            if step == 1:
+            if step == 0:
+                onward(h, d, 0).start()
+                continue
+            if step == 1 and h < NEAR:
                 audio_in(h, 1 - 2 * d)
             else:
                 onward(h, d, step - 1).wait_recv()
             if step < 4:
                 onward(h, d, step).start()
-        if step == 2:
+        if step == 2 and h < NEAR:
             audio_in(h, 0)
         if step > 1:
             spread(h, *SPREADS[step - 2])
@@ -371,7 +377,7 @@
         def _():
             awaited(pads.at[pl.ds(0, 2), 0], down_sent.at[i])
 
-    for sem, a, b in ((AUDIO, 3, 11), (VIDEO, 3, 24), (RING, 3, 20), (SUM, 3, 20), (QUERY, 3, 12), (HOME, 3, 11)):
+    for sem, a, b in ((AUDIO, 1, 17), (VIDEO, 3, 24), (RING, 4, 19), (SUM, 3, 20), (QUERY, 3, 12), (HOME, 3, 11)):
         awaited(pads.at[pl.ds(0, a), 0, pl.ds(0, b)], sem)
     awaited(lists_v.at[pl.ds(0, NX - 1)], LIST)
 
@@ -428,7 +434,7 @@
             pltpu.SMEM((2, TILES), jnp.int32),
             pltpu.VMEM((HPD, 2, 3, NX, ROWS, HDIM), BF16),
             *each(2, NX, 3, ROWS, HDIM),
-            sems(7), sems(2), sems(2), sems(HPD, 3), sems(HPD), sems(HPD, 2, 3), sems(HPD, 2),
+            sems(7), sems(2), sems(2), sems(HPD, 3), sems(HPD), sems(HPD, 2, 4), sems(HPD, 2),
             sems(HPD, 2, len(EDGES)), sems(HPD, 2, 3), sems(3), sems(HPD), sems(2),
         ],
         compiler_params=pltpu.CompilerParams(

time: 62.7 us -> 61.4 us (0.979)
  the two profiles are of different devices: /device:TPU:1 before, /device:TPU:8 now
where the time goes in v8:
time: 61.4 us; the launch traced here: 60.7 us
  Pallas kernels  60.1 us (98%)
  between operations  0.64 us (1%)
    pallas_call x1, Pallas kernels, per_device(): pl.pallas_call(kernel, out_shape=tuple((jax.ShapeDtypeStruct(a.shape, BF1...  58.1 us
    pallas_call x1, Pallas kernels, per_device(): pl.pallas_call(copy_kernel, out_shape=tuple((jax.ShapeDtypeStruct(a.shape...  2 us

profile of v8, /device:TPU:8, one launch (start us, length us, event | category | flops | bytes accessed | tf_op | source)
XLA Modules:
  0.0 60.7 jit_solution(15790066925785398918)
XLA Ops:
  0.6 58.1 %cross_attention_backward.1 = (bf16[256,1536]{1,0:T(8,128)(2,1)}, bf16[32,1536]{1,0:T(8,128)(2,1)}, bf16[32,1536]{1,0:T(8,128)(2,1)}) custom-call(bf16[256,1536]{1,0:T(8,128)(2,1)} %q.1, bf16[256,1536]{1,0:T(8,128)(2,1)} %g.1, bf16[32,1536]{1,0:T(8,128)(2,1)} %k.1, bf16[32,1536]{1,0:T(8,128)(2,1)} %v.1, s32[2,8]{1,0:T(2,128)} %lists.1), custom_call_target="tpu_custom_call" | custom-call | tf_op jit(solution)/shard_map/cross_attention_backward/pallas_call | solution.py:416
  58.7 2.0 %final_copies.1 = (bf16[256,1536]{1,0:T(8,128)(2,1)}, bf16[32,1536]{1,0:T(8,128)(2,1)}, bf16[32,1536]{1,0:T(8,128)(2,1)}) custom-call(bf16[256,1536]{1,0:T(8,128)(2,1)} %get-tuple-element.6.q, bf16[32,1536]{1,0:T(8,128)(2,1)} %get-tuple-element.7.k, bf16[32,1536]{1,0:T(8,128)(2,1)} %get-tuple-element.8.v), custom_call_target="tpu_custom_call" | custom-call | tf_op jit(solution)/shard_map/final_copies/pallas_call | solution.py:445

commit v9 on v8

--- a/solution.py
+++ b/solution.py
@@ -27,9 +27,9 @@
 
 SCHEDULE = (
     ("audio", 0), ("audio", 1), ("audio", 2), ("there", 1, 0), ("there", 2, 0), ("lists",), ("video", 0),
-    ("clear",), ("there", 0, 1), ("there", 1, 1), ("there", 2, 1),
-    ("video", 1), ("there", 0, 2), ("there", 1, 2), ("there", 2, 2), ("video", 2), ("there", 0, 3), ("there", 1, 3),
-    ("there", 2, 3), ("read",), ("there", 0, 4), ("there", 1, 4), ("there", 2, 4),
+    ("there", 0, 1), ("there", 1, 1), ("there", 2, 1), ("clear",),
+    ("video", 1), ("there", 0, 2), ("there", 1, 2), ("there", 2, 2), ("video", 2), ("read",), ("there", 0, 3), ("there", 1, 3),
+    ("there", 2, 3), ("there", 0, 4), ("there", 1, 4), ("there", 2, 4),
     ("compute", 0), ("compute", 1), ("compute", 2), ("edges", 0), ("edges", 1), ("edges", 2),
     ("back", 0, 4), ("back", 1, 4), ("back", 2, 4),
     ("back", 0, 3), ("back", 1, 3), ("back", 2, 3), ("back", 0, 2), ("back", 1, 2), ("back", 2, 2),

time: 61.4 us -> 61.4 us (level)
  no operation moved by 1% of the time
where the time goes in v9:
time: 61.4 us; the launch traced here: 60.7 us
  Pallas kernels  60.1 us (98%)
  between operations  0.64 us (1%)
    pallas_call x1, Pallas kernels, per_device(): pl.pallas_call(kernel, out_shape=tuple((jax.ShapeDtypeStruct(a.shape, BF1...  58.1 us
    pallas_call x1, Pallas kernels, per_device(): pl.pallas_call(copy_kernel, out_shape=tuple((jax.ShapeDtypeStruct(a.shape...  2 us

profile of v9, /device:TPU:8, one launch (start us, length us, event | category | flops | bytes accessed | tf_op | source)
XLA Modules:
  0.0 60.7 jit_solution(8742015469424999236)
XLA Ops:
  0.6 58.1 %cross_attention_backward.1 = (bf16[256,1536]{1,0:T(8,128)(2,1)}, bf16[32,1536]{1,0:T(8,128)(2,1)}, bf16[32,1536]{1,0:T(8,128)(2,1)}) custom-call(bf16[256,1536]{1,0:T(8,128)(2,1)} %q.1, bf16[256,1536]{1,0:T(8,128)(2,1)} %g.1, bf16[32,1536]{1,0:T(8,128)(2,1)} %k.1, bf16[32,1536]{1,0:T(8,128)(2,1)} %v.1, s32[2,8]{1,0:T(2,128)} %lists.1), custom_call_target="tpu_custom_call" | custom-call | tf_op jit(solution)/shard_map/cross_attention_backward/pallas_call | solution.py:416
  58.7 2.0 %final_copies.1 = (bf16[256,1536]{1,0:T(8,128)(2,1)}, bf16[32,1536]{1,0:T(8,128)(2,1)}, bf16[32,1536]{1,0:T(8,128)(2,1)}) custom-call(bf16[256,1536]{1,0:T(8,128)(2,1)} %get-tuple-element.6.q, bf16[32,1536]{1,0:T(8,128)(2,1)} %get-tuple-element.7.k, bf16[32,1536]{1,0:T(8,128)(2,1)} %get-tuple-element.8.v), custom_call_target="tpu_custom_call" | custom-call | tf_op jit(solution)/shard_map/final_copies/pallas_call | solution.py:445
